TPU v7x, 32 devices: a whole 2x2x4 slice. The times are simulated.
32 devices in a mesh: member: 4 (over y, x), lat: 2 (over core), lon: 4 (over z).
Axes of the slice: x: 2, y: 2, z: 4, core: 2. Of those that a mesh axis runs over, the one named last changes fastest.
Arguments:
- inputs: bfloat16 [4, 96, 2, 4, 23040], P('member', None, 'lat', 'lon'), may hold values from -6 to 6
- weight: bfloat16 [9, 8064], replicated, may hold values from -0.21875 to 0.21875
- bias: float32 [84], replicated, may hold values from -3 to 3
- analysis: bfloat16 [84, 2, 4, 23040], P(None, 'lat', 'lon'), may hold values from -7 to 7
- field_weight: float32 [84], replicated, may hold values from 0.25 to 2.5
Outputs:
- grad_input: bfloat16 [4, 96, 2, 4, 23040], P('member', None, 'lat', 'lon')
- grad_weight: float32 [9, 8064], replicated
- grad_bias: float32 [84], replicated
All inputs are finite; a program needn't handle non-finite values.
Results may differ from a plain program's by a relative error of at most 0.0053.
Values may be sent and summed in bfloat16 or wider, within the bound.
No kernel may reach another device: no remote copies, remote signals or barrier semaphores. Data moves between devices by JAX's collectives and lax.ppermute only.
A program may use at most 128 MiB of HBM per device.

v0:
```python
import jax
import jax.numpy as jnp
from jax import lax
from jax.sharding import PartitionSpec as P

LAT_DEV = 64


def with_halo(shard, sides, width, wrap):
    for axis, dim in sides:
        peers, length = (lax.axis_size(axis), shard.shape[dim])
        up = [(i, (i + 1) % peers) for i in range(peers if wrap else peers - 1)]
        down = [(j, i) for i, j in up]
        last = lax.slice_in_dim(shard, length - width, length, axis=dim)
        initial = lax.slice_in_dim(shard, 0, width, axis=dim)
        before = lax.ppermute(last, axis, up)
        after = lax.ppermute(initial, axis, down)
        shard = jnp.concatenate([before, shard, after], axis=dim)
    return shard


def kernel_slope(values):
    return values * lax.rsqrt(values * values + 1.0)


def extend(grid_field):
    lon_padded = with_halo(grid_field, (("lon", 2),), 1, True)
    return with_halo(lon_padded, (("lat", 1),), 1, False)


def local(inputs, weight, bias, analysis, field_weight):
    chan_count = inputs.shape[1]
    cell_count = inputs.shape[4]
    lat_count = LAT_DEV
    lon_count = cell_count // lat_count
    field_count = analysis.shape[0]
    grid_field = inputs[0, :, 0, 0].reshape(chan_count, lat_count, lon_count)
    target_grid = analysis[:, 0, 0].reshape(field_count, lat_count, lon_count)
    members = lax.axis_size("member")
    tap_weights = weight.reshape(9, chan_count, field_count)
    padded = extend(grid_field)
    summed_terms = jnp.zeros((field_count, cell_count), jnp.float32)
    windows = []
    for tap_index in range(9):
        row_off = tap_index // 3
        col_off = tap_index % 3
        window = padded[:, row_off : row_off + lat_count, col_off : col_off + lon_count].reshape(
            chan_count, cell_count
        )
        windows.append(window)
        summed_terms = summed_terms + jnp.dot(
            tap_weights[tap_index].T, window, preferred_element_type=jnp.float32
        )
    summed_terms = summed_terms + bias[:, None]
    prediction = summed_terms.astype(jnp.bfloat16).reshape(field_count, lat_count, lon_count)
    scale_field = field_weight[:, None, None]
    quarter_rows = lat_count // members
    by_cells = lax.all_to_all(prediction[None], "member", split_axis=2, concat_axis=0, tiled=True)
    row_start = lax.axis_index("member") * quarter_rows
    target_rows = lax.dynamic_slice_in_dim(target_grid, row_start, quarter_rows, 1).astype(
        jnp.float32
    )
    member_values = by_cells.astype(jnp.float32)
    pair_slope = jnp.sum(kernel_slope(member_values[:, None] - member_values[None, :]), axis=1)
    target_slope = kernel_slope(member_values - target_rows[None])
    cell_grad = (
        scale_field[None] * (target_slope / members - pair_slope / (members * (members - 1)))
    ).astype(jnp.bfloat16)
    returned = lax.all_to_all(cell_grad, "member", split_axis=0, concat_axis=2, tiled=True)
    pred_grad = returned[0]
    grad_padded = extend(pred_grad)
    grad_flat = pred_grad.reshape(field_count, cell_count)
    input_terms = jnp.zeros((chan_count, cell_count), jnp.float32)
    weight_terms = []
    for tap_index in range(9):
        row_off = tap_index // 3
        col_off = tap_index % 3
        weight_terms.append(
            lax.dot_general(
                windows[tap_index],
                grad_flat,
                (((1,), (1,)), ((), ())),
                preferred_element_type=jnp.float32,
            )
        )
        grad_window = grad_padded[
            :, 2 - row_off : 2 - row_off + lat_count, 2 - col_off : 2 - col_off + lon_count
        ].reshape(field_count, cell_count)
        input_terms = input_terms + jnp.dot(
            tap_weights[tap_index], grad_window, preferred_element_type=jnp.float32
        )
    bias_terms = jnp.sum(grad_flat.astype(jnp.float32), axis=1)
    weight_total, bias_total = lax.psum(
        (jnp.stack(weight_terms), bias_terms), ("member", "lat", "lon")
    )
    global_cells = cell_count * lax.axis_size("lat") * lax.axis_size("lon")
    grad_input = input_terms.astype(jnp.bfloat16).reshape(1, chan_count, 1, 1, cell_count)
    grad_weight = (weight_total / global_cells).reshape(9, chan_count * field_count)
    grad_bias = bias_total / global_cells
    return (grad_input, grad_weight, grad_bias)


def solution(mesh):
    placed = (P("member", None, "lat", "lon", None), P(), P(), P(None, "lat", "lon", None), P())
    return jax.shard_map(
        local,
        mesh=mesh,
        in_specs=placed,
        out_specs=(P("member", None, "lat", "lon", None), P(), P()),
        check_vma=False,
    )
```

profile of v0, /device:TPU:0, one launch (start us, length us, event | category | flops | bytes accessed | tf_op | source)
XLA Modules:
  0.0 593.8 jit_solution(433074452347337279)
XLA Ops:
  7.2 14.2 %reshape_squeeze.10 = bf16[96,64,360]{2,1,0:T(8,128)(2,1)} reshape(bf16[1,96,1,1,23040]{4,1,3,2,0:T(8,128)(2,1)} %param.5) | data formatting | bytes 8847360 | tf_op jit(solution)/shard_map/reshape;squeeze | solution.py:37
  44.0 7.6 %pad_maximum_fusion.2 = (bf16[96,64,360]{2,1,0:T(8,128)(2,1)}, bf16[96,64,360]{2,1,0:T(8,128)(2,1)}) fusion(bf16[96,64,360]{2,1,0:T(8,128)(2,1)S(1)} %bitcast.151, bf16[96,64,1]{2,1,0:T(8,128)(2,1)S(1)} %copy.49, bf16[96,64,1]{2,1,0:T(8,128)(2,1)S(1)} %copy-done.8), kind=kLoop, calls=%fused_computation.36 | loop fusion | flops 17694720 | bytes 13295616 | tf_op jit(solution)/shard_map/concatenate | solution.py:18
  54.6 9.5 %reshape.99 = bf16[96,23040]{1,0:T(8,128)(2,1)} reshape(bf16[96,64,360]{2,1,0:T(8,128)(2,1)} %get-tuple-element.27) | data formatting | bytes 8847360 | tf_op jit(solution)/shard_map/reshape | solution.py:47
  64.1 6.7 %convolution_bitcast_fusion.3 = f32[84,23040]{1,0:T(8,128)} fusion(bf16[96,23040]{1,0:T(8,128)(2,1)} %reshape.99, bf16[96,84]{1,0:T(8,128)(2,1)S(1)} %squeeze.44), kind=kOutput, calls=%fused_computation.26 | convolution fusion | flops 371589120 | bytes 12181248 | tf_op jit(solution)/shard_map/dot_general | solution.py:51
  70.8 9.5 %reshape.98 = bf16[96,23040]{1,0:T(8,128)(2,1)} reshape(bf16[96,64,360]{2,1,0:T(8,128)(2,1)} %get-tuple-element.26) | data formatting | bytes 8847360 | tf_op jit(solution)/shard_map/reshape | solution.py:47
  80.3 14.4 %maximum_maximum_fusion = (bf16[96,65,362]{2,1,0:T(8,128)(2,1)S(1)}, bf16[96,65,362]{2,1,0:T(8,128)(2,1)S(1)}) fusion(bf16[96,64,1]{2,1,0:T(8,128)(2,1)} %copy.50, bf16[96,64,360]{2,1,0:T(8,128)(2,1)} %reshape_squeeze.10, bf16[96,64,1]{2,1,0:T(8,128)(2,1)S(1)} %copy.49, bf16[96,1,362]{2,1,0:T(2,128)(2,1)S(1)} %collective-permute-done.2, ...), kind=kLoop, calls=%fused_computation.33 | loop fusion | flops 36142080 | bytes 13622784 | tf_op jit(solution)/shard_map/concatenate | solution.py:18
  94.7 13.4 %fusion.29 = (bf16[96,64,360]{2,1,0:T(8,128)(2,1)}, bf16[96,64,360]{2,1,0:T(8,128)(2,1)}, bf16[96,64,360]{2,1,0:T(8,128)(2,1)}, bf16[96,64,360]{2,1,0:T(8,128)(2...) fusion(bf16[96,65,362]{2,1,0:T(8,128)(2,1)S(1)} %get-tuple-element.13, ...), kind=kLoop, calls=%fused_computation.81 | loop fusion | bytes 53084160 | tf_op jit(solution)/shard_map/slice | solution.py:47
  108.1 9.5 %reshape.96 = bf16[96,23040]{1,0:T(8,128)(2,1)} reshape(bf16[96,64,360]{2,1,0:T(8,128)(2,1)} %get-tuple-element.43) | data formatting | bytes 8847360 | tf_op jit(solution)/shard_map/reshape | solution.py:47
  117.6 19.9 %reshape.95 = bf16[96,23040]{1,0:T(8,128)(2,1)} reshape(bf16[96,64,360]{2,1,0:T(8,128)(2,1)} %get-tuple-element.42) | data formatting | bytes 8847360 | tf_op jit(solution)/shard_map/reshape | solution.py:47
  137.5 9.5 %reshape.97 = bf16[96,23040]{1,0:T(8,128)(2,1)} reshape(bf16[96,64,360]{2,1,0:T(8,128)(2,1)} %get-tuple-element.44) | data formatting | bytes 8847360 | tf_op jit(solution)/shard_map/reshape | solution.py:47
  147.0 9.5 %reshape.100 = bf16[96,23040]{1,0:T(8,128)(2,1)} reshape(bf16[96,64,360]{2,1,0:T(8,128)(2,1)} %get-tuple-element.22) | data formatting | bytes 8847360 | tf_op jit(solution)/shard_map/reshape | solution.py:47
  156.5 9.5 %reshape.101 = bf16[96,23040]{1,0:T(8,128)(2,1)} reshape(bf16[96,64,360]{2,1,0:T(8,128)(2,1)} %get-tuple-element.21) | data formatting | bytes 8847360 | tf_op jit(solution)/shard_map/reshape | solution.py:47
  166.0 9.5 %reshape.102 = bf16[96,23040]{1,0:T(8,128)(2,1)} reshape(bf16[96,64,360]{2,1,0:T(8,128)(2,1)} %get-tuple-element.20) | data formatting | bytes 8847360 | tf_op jit(solution)/shard_map/reshape | solution.py:47
  175.5 3.7 fusion.35
  179.2 6.8 %convolution_bitcast_fusion.2 = f32[84,23040]{1,0:T(8,128)} fusion(bf16[96,23040]{1,0:T(8,128)(2,1)} %reshape.100, bf16[96,84]{1,0:T(8,128)(2,1)S(1)} %squeeze.45), kind=kOutput, calls=%fused_computation.25 | convolution fusion | flops 371589120 | bytes 12181248 | tf_op jit(solution)/shard_map/dot_general | solution.py:51
  190.1 12.6 %fusion.4 = f32[84,23040]{1,0:T(8,128)} fusion(f32[84,23040]{1,0:T(8,128)} %convolution_bitcast_fusion.2, f32[84,23040]{1,0:T(8,128)} %convolution_bitcast_fusion.3, f32[84,23040]{1,0:T(8,128)S(1)} %fusion.5, bf16[96,84]{1,0:T(8,128)(2,1)S(1)} %squeeze.43, bf16[1,96,1,1,23040]{4,1,3,2,0:T(8,128)(2,1)} %param.5), kind=kOutput, calls=%fused_computation.15 | convolution fusion | flops 377395200 | bytes 35405568 | tf_op jit(solution)/shard_map/dot_general | solution.py:51
  202.8 4.5 fusion.8
  207.4 3.5 fusion.10
  210.9 12.9 %broadcast_in_dim_reshape.3 = bf16[1,84,64,360]{3,2,1,0:T(8,128)(2,1)} reshape(bf16[84,23040]{1,0:T(8,128)(2,1)} %fusion.10) | data formatting | bytes 7741440 | tf_op jit(solution)/shard_map/broadcast_in_dim;reshape | solution.py:58
  223.8 6.6 %copy.53 = bf16[1,84,64,360]{3,1,0,2:T(8,128)(2,1)} copy(bf16[1,84,64,360]{3,2,1,0:T(8,128)(2,1)} %broadcast_in_dim_reshape.3) | data formatting | bytes 7741440 | tf_op jit(solution)/shard_map/broadcast_in_dim;reshape | solution.py:58
  230.4 4.9 all-to-all-start
  235.4 12.5 %reshape_squeeze.11 = bf16[84,64,360]{2,1,0:T(8,128)(2,1)} reshape(bf16[84,1,1,23040]{3,0,2,1:T(8,128)(2,1)} %param.8) | data formatting | bytes 7741440 | tf_op jit(solution)/shard_map/reshape;squeeze | solution.py:38
  249.3 36.1 %all-to-all-done = bf16[1,84,64,360]{3,1,0,2:T(8,128)(2,1)} async-done(((bf16[1,84,64,360]{3,1,0,2:T(8,128)(2,1)}), bf16[1,84,64,360]{3,1,0,2:T(8,128)(2,1)}, u32[]{:S(2)}, u32[]{:S(2)}) %all-to-all-start) | async-done | bytes 3870752 | tf_op jit(solution)/shard_map/all_to_all | solution.py:58
  289.1 7.9 %fusion.2 = f32[4,84,16,360]{3,2,1,0:T(8,128)S(1)} fusion(f32[4,84,16,360]{3,2,1,0:T(8,128)S(1)} %copy_bitcast_fusion), kind=kLoop, calls=%fused_computation.4 | loop fusion | flops 36771840 | bytes 15482880 | tf_op jit(solution)/shard_map/reduce_sum | solution.py:64
  300.2 50.6 %all_to_all.24 = bf16[4,84,16,360]{3,2,1,0:T(8,128)(2,1)S(1)} all-to-all(bf16[4,84,16,360]{3,2,1,0:T(8,128)(2,1)S(1)} %multiply_convert_fusion), channel_id=1, replica_groups=mesh['member'=4,'lat'=2,'lon'=4] {'member'}, dimensions={0} | all-to-all | bytes 7741440 | tf_op jit(solution)/shard_map/all_to_all | solution.py:69
  354.1 8.4 %reshape_squeeze.12 = bf16[84,23040]{1,0:T(8,128)(2,1)} reshape(bf16[1,84,4,16,360]{4,3,2,1,0:T(8,128)(2,1)} %bitcast.145) | data formatting | bytes 7741440 | tf_op jit(solution)/shard_map/reshape;squeeze | solution.py:88
  362.5 4.9 fusion.28
  367.4 3.7 fusion.27
  389.2 3.8 collective-permute-start.5
  396.1 36.9 %psum.15 = f32[84]{0:T(128)S(1)} all-reduce(f32[84]{0:T(128)S(1)} %convert_reduce_fusion), channel_id=1, replica_groups=mesh['member'=4,'lat'=2,'lon'=4] {'member','lat','lon'}, use_global_device_ids=true, to_apply=%region_3.0 | all-reduce | flops 84 | bytes 672 | tf_op jit(solution)/shard_map/psum | solution.py:93
  441.6 3.4 collective-permute-start.7
  445.1 7.3 %pad_maximum_fusion.4 = (bf16[84,64,360]{2,1,0:T(8,128)(2,1)}, bf16[84,64,360]{2,1,0:T(8,128)(2,1)}) fusion(bf16[84,64,360]{2,1,0:T(8,128)(2,1)S(1)} %bitcast.149, bf16[84,64,1]{2,1,0:T(8,128)(2,1)S(1)} %copy.59, bf16[84,64,1]{2,1,0:T(8,128)(2,1)S(1)} %copy.60), kind=kLoop, calls=%fused_computation.42 | loop fusion | flops 15482880 | bytes 11633664 | tf_op jit(solution)/shard_map/concatenate | solution.py:18
  452.4 8.3 %reshape.106 = bf16[84,23040]{1,0:T(8,128)(2,1)} reshape(bf16[84,64,360]{2,1,0:T(8,128)(2,1)} %get-tuple-element.37) | data formatting | bytes 7741440 | tf_op jit(solution)/shard_map/reshape | solution.py:88
  460.7 8.3 %reshape.107 = bf16[84,23040]{1,0:T(8,128)(2,1)} reshape(bf16[84,64,360]{2,1,0:T(8,128)(2,1)} %get-tuple-element.36) | data formatting | bytes 7741440 | tf_op jit(solution)/shard_map/reshape | solution.py:88
  469.0 13.2 %maximum_maximum_fusion.1 = (bf16[84,65,362]{2,1,0:T(8,128)(2,1)}, bf16[84,65,362]{2,1,0:T(8,128)(2,1)S(1)}) fusion(bf16[84,64,1]{2,1,0:T(8,128)(2,1)S(1)} %copy.60, bf16[84,64,360]{2,1,0:T(8,128)(2,1)} %bitcast.148, bf16[84,64,1]{2,1,0:T(8,128)(2,1)S(1)} %copy.59, bf16[84,1,362]{2,1,0:T(2,128)(2,1)S(1)} %collective-permute-done.7, ...), kind=kLoop, calls=%fused_computation.38 | loop fusion | flops 31624320 | bytes 11919936 | tf_op jit(solution)/shard_map/concatenate | solution.py:18
  482.2 8.6 %fusion.33 = (bf16[84,64,360]{2,1,0:T(8,128)(2,1)}, bf16[84,64,360]{2,1,0:T(8,128)(2,1)}, bf16[84,64,360]{2,1,0:T(8,128)(2,1)}) fusion(bf16[84,65,362]{2,1,0:T(8,128)(2,1)S(1)} %get-tuple-element.17), kind=kLoop, calls=%fused_computation.85 | loop fusion | bytes 23224320 | tf_op jit(solution)/shard_map/slice | solution.py:86
  490.9 8.3 %reshape.104 = bf16[84,23040]{1,0:T(8,128)(2,1)} reshape(bf16[84,64,360]{2,1,0:T(8,128)(2,1)} %get-tuple-element.34) | data formatting | bytes 7741440 | tf_op jit(solution)/shard_map/reshape | solution.py:88
  499.2 6.9 %fusion.36 = f32[23040,96]{0,1:T(8,128)} fusion(bf16[84,23040]{1,0:T(8,128)(2,1)} %reshape.104, bf16[96,84]{1,0:T(8,128)(2,1)S(1)} %squeeze.40), kind=kOutput, calls=%fused_computation.88 | convolution fusion | flops 371589120 | bytes 12734208 | tf_op jit(solution)/shard_map/dot_general | solution.py:89
  506.1 8.3 %reshape.103 = bf16[84,23040]{1,0:T(8,128)(2,1)} reshape(bf16[84,64,360]{2,1,0:T(8,128)(2,1)} %get-tuple-element.35) | data formatting | bytes 7741440 | tf_op jit(solution)/shard_map/reshape | solution.py:88
  514.4 8.5 %reshape.105 = bf16[84,23040]{1,0:T(8,128)(2,1)} reshape(bf16[84,64,360]{2,1,0:T(8,128)(2,1)} %get-tuple-element.33) | data formatting | bytes 7741440 | tf_op jit(solution)/shard_map/reshape | solution.py:88
  522.9 6.2 %convolution_add_fusion.7 = f32[23040,96]{0,1:T(8,128)S(1)} fusion(f32[23040,96]{0,1:T(8,128)} %fusion.36, bf16[84,23040]{1,0:T(8,128)(2,1)} %reshape.103, bf16[96,84]{1,0:T(8,128)(2,1)S(1)} %squeeze.39), kind=kOutput, calls=%fused_computation.12 | convolution fusion | flops 373800960 | bytes 21581568 | tf_op jit(solution)/shard_map/dot_general | solution.py:89
  530.4 3.6 convolution_add_fusion.5
  534.1 4.8 convolution_add_fusion.4
  538.9 6.1 %fusion.32 = (bf16[84,64,360]{2,1,0:T(8,128)(2,1)}, bf16[84,64,360]{2,1,0:T(8,128)(2,1)}, bf16[84,64,360]{2,1,0:T(8,128)(2,1)}) fusion(bf16[84,65,362]{2,1,0:T(8,128)(2,1)S(1)} %bitcast.153), kind=kLoop, calls=%fused_computation.84 | loop fusion | bytes 23224320 | tf_op jit(solution)/shard_map/slice | solution.py:86
  545.0 8.3 %reshape.108 = bf16[84,23040]{1,0:T(8,128)(2,1)} reshape(bf16[84,64,360]{2,1,0:T(8,128)(2,1)} %get-tuple-element.32) | data formatting | bytes 7741440 | tf_op jit(solution)/shard_map/reshape | solution.py:88
  553.3 8.3 %reshape.109 = bf16[84,23040]{1,0:T(8,128)(2,1)} reshape(bf16[84,64,360]{2,1,0:T(8,128)(2,1)} %get-tuple-element.31) | data formatting | bytes 7741440 | tf_op jit(solution)/shard_map/reshape | solution.py:88
  561.6 8.5 %reshape.110 = bf16[84,23040]{1,0:T(8,128)(2,1)} reshape(bf16[84,64,360]{2,1,0:T(8,128)(2,1)} %get-tuple-element.30) | data formatting | bytes 7741440 | tf_op jit(solution)/shard_map/reshape | solution.py:88
  570.2 6.2 %convolution_add_fusion.3 = f32[23040,96]{0,1:T(8,128)S(1)} fusion(f32[23040,96]{0,1:T(8,128)} %convolution_add_fusion.4, bf16[84,23040]{1,0:T(8,128)(2,1)} %reshape.107, bf16[96,84]{1,0:T(8,128)(2,1)S(1)} %copy-done.18), kind=kOutput, calls=%fused_computation.8 | convolution fusion | flops 373800960 | bytes 21581568 | tf_op jit(solution)/shard_map/dot_general | solution.py:89
  (175 shorter events, 82.1 us)
Async XLA Ops:
  21.4 11.2 %copy-start.10 = (bf16[9,8064]{1,0:T(8,128)(2,1)S(1)}, bf16[9,8064]{1,0:T(8,128)(2,1)}, u32[]{:S(2)}) copy-start(bf16[9,8064]{1,0:T(8,128)(2,1)} %param.6) | copy-start | bytes 435460
  25.7 8.9 %collective-permute-start = (bf16[96,64,1]{0,1,2:T(8,128)(2,1)S(1)}, bf16[96,64,1]{0,1,2:T(8,128)(2,1)S(1)}, u32[]{:S(2)}, u32[]{:S(2)}) collective-permute-start(bf16[96,64,1]{0,1,2:T(8,128)(2,1)S(1)} %copy.47), channel_id=1, source_target_pairs={{0,1},{1,2},{2,3},{3,0},{4,5},{5,6},{6,7},{7,4},{8,9},{9,10},{10,1... | collective-permute-start | bytes 36872 | tf_op jit(solution)/shard_map/ppermute | solution.py:16
  30.5 6.9 %collective-permute-start.1 = (bf16[96,64,1]{0,1,2:T(8,128)(2,1)S(1)}, bf16[96,64,1]{0,1,2:T(8,128)(2,1)S(1)}, u32[]{:S(2)}, u32[]{:S(2)}) collective-permute-start(bf16[96,64,1]{0,1,2:T(8,128)(2,1)S(1)} %copy.48), channel_id=1, source_target_pairs={{1,0},{2,1},{3,2},{0,3},{5,4},{6,5},{7,6},{4,7},{9,8},{10,9},{11,1... | collective-permute-start | bytes 36872 | tf_op jit(solution)/shard_map/ppermute | solution.py:17
  34.0 145.1 %copy-start.15 = (bf16[96,84]{1,0:T(8,128)(2,1)}, bf16[96,84]{1,0:T(8,128)(2,1)S(1)}, u32[]{:S(2)}) copy-start(bf16[96,84]{1,0:T(8,128)(2,1)S(1)} %squeeze.45) | copy-start | bytes 48388
  34.2 29.9 %copy-start.17 = (bf16[96,84]{1,0:T(8,128)(2,1)}, bf16[96,84]{1,0:T(8,128)(2,1)S(1)}, u32[]{:S(2)}) copy-start(bf16[96,84]{1,0:T(8,128)(2,1)S(1)} %squeeze.44) | copy-start | bytes 48388
  34.5 168.3 %copy-start.13 = (bf16[96,84]{1,0:T(8,128)(2,1)}, bf16[96,84]{1,0:T(8,128)(2,1)S(1)}, u32[]{:S(2)}) copy-start(bf16[96,84]{1,0:T(8,128)(2,1)S(1)} %squeeze.46) | copy-start | bytes 48388
  34.6 172.7 %copy-start.11 = (bf16[96,84]{1,0:T(8,128)(2,1)}, bf16[96,84]{1,0:T(8,128)(2,1)S(1)}, u32[]{:S(2)}) copy-start(bf16[96,84]{1,0:T(8,128)(2,1)S(1)} %squeeze.47) | copy-start | bytes 48388
  37.4 5.9 slice-start
  40.7 2.8 slice-start.1
  40.7 3.2 copy-start.8
  51.6 28.7 %collective-permute-start.2 = (bf16[96,1,362]{2,1,0:T(2,128)(2,1)S(1)}, bf16[96,1,362]{2,1,0:T(2,128)(2,1)S(1)}, u32[]{:S(2)}, u32[]{:S(2)}) collective-permute-start(bf16[96,1,362]{2,1,0:T(2,128)(2,1)S(1)} %get-tuple-element.14), channel_id=1, source_target_pairs={{0,4},{1,5},{2,6},{3,7},{8,12},{9,13},{10,14},{11,15},{16,20},{17,... | collective-permute-start | bytes 208520 | tf_op jit(solution)/shard_map/ppermute | solution.py:16
  53.1 27.2 %collective-permute-start.3 = (bf16[96,1,362]{2,1,0:T(2,128)(2,1)S(1)}, bf16[96,1,362]{2,1,0:T(2,128)(2,1)S(1)}, u32[]{:S(2)}, u32[]{:S(2)}) collective-permute-start(bf16[96,1,362]{2,1,0:T(2,128)(2,1)S(1)} %get-tuple-element.15), channel_id=1, source_target_pairs={{4,0},{5,1},{6,2},{7,3},{12,8},{13,9},{14,10},{15,11},{20,16},{21,... | collective-permute-start | bytes 208520 | tf_op jit(solution)/shard_map/ppermute | solution.py:17
  166.0 20.0 %slice-start.20 = ((s8[4423680]{0:T(1024)(128)(4,1)}), s8[229376]{0:T(1024)(128)(4,1)S(1)}, s32[]{:S(2)}) async-start(s8[4423680]{0:T(1024)(128)(4,1)} %bitcast.170), calls=%async_computation.23 | async-start | bytes 458752
  175.5 10.5 %slice-start.21 = ((s8[4423680]{0:T(1024)(128)(4,1)}), s8[4194304]{0:T(1024)(128)(4,1)S(1)}, s32[]{:S(2)}) async-start(s8[4423680]{0:T(1024)(128)(4,1)} %bitcast.170), calls=%async_computation.24 | async-start | bytes 8388608
  179.2 8.2 %slice-start.16 = ((s8[4423680]{0:T(1024)(128)(4,1)}), s8[4194304]{0:T(1024)(128)(4,1)S(1)}, s32[]{:S(2)}) async-start(s8[4423680]{0:T(1024)(128)(4,1)} %bitcast.166), calls=%async_computation.19 | async-start | bytes 8388608
  186.0 2.8 slice-start.8
  188.8 14.0 %slice-start.12 = ((s8[4423680]{0:T(1024)(128)(4,1)}), s8[229376]{0:T(1024)(128)(4,1)S(1)}, s32[]{:S(2)}) async-start(s8[4423680]{0:T(1024)(128)(4,1)} %bitcast.162), calls=%async_computation.15 | async-start | bytes 458752
  188.8 18.6 %slice-start.4 = ((s8[4423680]{0:T(1024)(128)(4,1)}), s8[229376]{0:T(1024)(128)(4,1)S(1)}, s32[]{:S(2)}) async-start(s8[4423680]{0:T(1024)(128)(4,1)} %bitcast.154), calls=%async_computation.7 | async-start | bytes 458752
  190.1 12.6 %slice-start.13 = ((s8[4423680]{0:T(1024)(128)(4,1)}), s8[4194304]{0:T(1024)(128)(4,1)S(1)}, s32[]{:S(2)}) async-start(s8[4423680]{0:T(1024)(128)(4,1)} %bitcast.162), calls=%async_computation.16 | async-start | bytes 8388608
  190.1 17.2 %slice-start.5 = ((s8[4423680]{0:T(1024)(128)(4,1)}), s8[4194304]{0:T(1024)(128)(4,1)S(1)}, s32[]{:S(2)}) async-start(s8[4423680]{0:T(1024)(128)(4,1)} %bitcast.154), calls=%async_computation.8 | async-start | bytes 8388608
  202.8 4.6 copy-start.19
  230.4 54.9 %all-to-all-start = ((bf16[1,84,64,360]{3,1,0,2:T(8,128)(2,1)}), bf16[1,84,64,360]{3,1,0,2:T(8,128)(2,1)}, u32[]{:S(2)}, u32[]{:S(2)}) async-start(bf16[1,84,64,360]{3,1,0,2:T(8,128)(2,1)} %copy.53), calls=%async_computation | async-start | bytes 8650752 | tf_op jit(solution)/shard_map/all_to_all | solution.py:58
  235.3 348.8 %all-reduce.2.cloned.1.call-start = ((), (), s32[]{:S(2)}) async-start(), calls=%async_computation.2 | async-start | bytes 811008 | tf_op jit(solution)/shard_map/psum | solution.py:93
  289.1 8.0 %copy-start.20 = (f32[84]{0:T(128)S(1)}, f32[84]{0:T(128)}, u32[]{:S(2)}) copy-start(f32[84]{0:T(128)} %param.9) | copy-start | bytes 1012
  350.8 3.3 copy-start.3
  354.1 17.0 %slice-start.18 = ((s8[4423680]{0:T(1024)(128)(4,1)}), s8[229376]{0:T(1024)(128)(4,1)S(1)}, s32[]{:S(2)}) async-start(s8[4423680]{0:T(1024)(128)(4,1)} %bitcast.168), calls=%async_computation.21 | async-start | bytes 458752
  362.5 4.9 copy-start
  362.5 8.7 %slice-start.19 = ((s8[4423680]{0:T(1024)(128)(4,1)}), s8[4194304]{0:T(1024)(128)(4,1)S(1)}, s32[]{:S(2)}) async-start(s8[4423680]{0:T(1024)(128)(4,1)} %bitcast.168), calls=%async_computation.22 | async-start | bytes 8388608
  367.4 5.1 slice-start.10
  371.2 2.7 slice-start.26
  371.2 5.0 slice-start.22
  372.6 3.6 slice-start.23
  374.9 2.7 slice-start.24
  374.9 4.9 slice-start.14
  376.2 3.6 slice-start.15
  378.5 2.7 slice-start.6
  387.3 46.2 %collective-permute-start.4 = (bf16[84,64,1]{0,1,2:T(8,128)(2,1)S(1)}, bf16[84,64,1]{0,1,2:T(8,128)(2,1)S(1)}, u32[]{:S(2)}, u32[]{:S(2)}) collective-permute-start(bf16[84,64,1]{0,1,2:T(8,128)(2,1)S(1)} %copy.57), channel_id=1, source_target_pairs={{0,1},{1,2},{2,3},{3,0},{4,5},{5,6},{6,7},{7,4},{8,9},{9,10},{10,1... | collective-permute-start | bytes 32264 | tf_op jit(solution)/shard_map/ppermute | solution.py:16
  389.2 46.7 %collective-permute-start.5 = (bf16[84,64,1]{0,1,2:T(8,128)(2,1)S(1)}, bf16[84,64,1]{0,1,2:T(8,128)(2,1)S(1)}, u32[]{:S(2)}, u32[]{:S(2)}) collective-permute-start(bf16[84,64,1]{0,1,2:T(8,128)(2,1)S(1)} %copy.58), channel_id=1, source_target_pairs={{1,0},{2,1},{3,2},{0,3},{5,4},{6,5},{7,6},{4,7},{9,8},{10,9},{11,1... | collective-permute-start | bytes 32264 | tf_op jit(solution)/shard_map/ppermute | solution.py:17
  438.2 6.9 %copy-start.2 = (bf16[4,84,16,360]{3,2,0,1:T(8,128)(2,1)S(1)}, bf16[4,84,16,360]{3,2,0,1:T(8,128)(2,1)}, u32[]{:S(2)}) copy-start(bf16[4,84,16,360]{3,2,0,1:T(8,128)(2,1)} %copy.70) | copy-start | bytes 11612164
  440.3 28.7 %collective-permute-start.6 = (bf16[84,1,362]{2,1,0:T(2,128)(2,1)S(1)}, bf16[84,1,362]{2,1,0:T(2,128)(2,1)S(1)}, u32[]{:S(2)}, u32[]{:S(2)}) collective-permute-start(bf16[84,1,362]{2,1,0:T(2,128)(2,1)S(1)} %get-tuple-element.19), channel_id=1, source_target_pairs={{4,0},{5,1},{6,2},{7,3},{12,8},{13,9},{14,10},{15,11},{20,16},{21,... | collective-permute-start | bytes 182456 | tf_op jit(solution)/shard_map/ppermute | solution.py:17
  441.6 27.4 %collective-permute-start.7 = (bf16[84,1,362]{2,1,0:T(2,128)(2,1)S(1)}, bf16[84,1,362]{2,1,0:T(2,128)(2,1)S(1)}, u32[]{:S(2)}, u32[]{:S(2)}) collective-permute-start(bf16[84,1,362]{2,1,0:T(2,128)(2,1)S(1)} %get-tuple-element.18), channel_id=1, source_target_pairs={{0,4},{1,5},{2,6},{3,7},{8,12},{9,13},{10,14},{11,15},{16,20},{17,... | collective-permute-start | bytes 182456 | tf_op jit(solution)/shard_map/ppermute | solution.py:16
  522.9 6.2 %copy-start.7 = (bf16[84,23040]{1,0:T(8,128)(2,1)S(1)}, bf16[84,23040]{1,0:T(8,128)(2,1)}, u32[]{:S(2)}) copy-start(bf16[84,23040]{1,0:T(8,128)(2,1)} %reshape.105) | copy-start | bytes 11612164
  530.4 3.6 copy-start.1
  530.4 8.4 %slice-start.2 = ((s8[4644864]{0:T(1024)(128)(4,1)}), s8[4194304]{0:T(1024)(128)(4,1)S(1)}, s32[]{:S(2)}) async-start(s8[4644864]{0:T(1024)(128)(4,1)} %bitcast.152), calls=%async_computation.5 | async-start | bytes 8388608
  534.1 4.8 slice-start.3
  561.6 8.6 %copy-start.18 = (bf16[96,84]{1,0:T(8,128)(2,1)S(1)}, bf16[96,84]{1,0:T(8,128)(2,1)}, u32[]{:S(2)}) copy-start(bf16[96,84]{1,0:T(8,128)(2,1)} %copy-done.17) | copy-start | bytes 48388
  570.2 6.2 %copy-start.6 = (bf16[84,23040]{1,0:T(8,128)(2,1)S(1)}, bf16[84,23040]{1,0:T(8,128)(2,1)}, u32[]{:S(2)}) copy-start(bf16[84,23040]{1,0:T(8,128)(2,1)} %reshape.108) | copy-start | bytes 11612164
  570.2 6.2 %copy-start.16 = (bf16[96,84]{1,0:T(8,128)(2,1)S(1)}, bf16[96,84]{1,0:T(8,128)(2,1)}, u32[]{:S(2)}) copy-start(bf16[96,84]{1,0:T(8,128)(2,1)} %copy-done.15) | copy-start | bytes 48388
  (11 other events, 19.4 us)
Sparse Core Ops, SparseCore 0:
  383.4 123.7 all-reduce.1
where the time goes:
time: 605 us; the launch traced here: 594 us
  local copies, waits for them, and re-layouts  273 us (45%)
  matrix products  94.8 us (16%)
  blocking collectives  87.5 us (14%)
  other arithmetic  65.1 us (11%)
  waiting for transfers between devices  36.1 us (6%)
  starting transfers between devices  21.9 us (4%)
  between operations  15.5 us (3%)
    reshape x8, local copies, waits for them, and re-layouts, local(): padded[:, row_off:row_off + lat_count, col_off:col_off + lon_count]  86.3 us
    reshape x8, local copies, waits for them, and re-layouts, local(): grad_window = grad_padded[:, 2 - row_off:2 - row_off + lat_count, 2 - col...  66.9 us
    all_to_all x1, blocking collectives, local(): lax.all_to_all(cell_grad, 'member', split_axis=0, concat_axis=2, tiled=True)  50.6 us
    concatenate x5, other arithmetic, with_halo(): shard = jnp.concatenate([before, shard, after], axis=dim)  44.7 us
    dot_general x9, matrix products, local(): jnp.dot(tap_weights[tap_index].T, window, preferred_element_type=jnp.floa...  41.8 us
    psum x1, blocking collectives, local(): lax.psum((jnp.stack(weight_terms), bias_terms), ('member', 'lat', 'lon'))  36.9 us
    all_to_all x1, waiting for transfers between devices, local(): lax.all_to_all(prediction[None], 'member', split_axis=2, concat_axis=0, t...  36.1 us
    dot_general x9, matrix products, local(): jnp.dot(tap_weights[tap_index], grad_window, preferred_element_type=jnp.f...  35.2 us
  transfers between devices with their start and end apart: 10, of which 1 were waited for; matrix products, arithmetic and copies ran while one was open for 34% of the time, Pallas kernels for 0%

commit v1 on v0

v1 whole, which is shorter than its diff:
```python
import functools

import jax
import jax.numpy as jnp
from jax import lax
from jax.experimental import pallas as pl
from jax.experimental.pallas import tpu as pltpu
from jax.sharding import PartitionSpec as P

LAT_DEV = 64
LANES = 128
TILE = 512
VMEM_LIMIT = 56 * 1024 * 1024
F32 = jnp.float32
BF16 = jnp.bfloat16


def round_up(value, step):
    return -(-value // step) * step


def params():
    return pltpu.CompilerParams(vmem_limit_bytes=VMEM_LIMIT)


def shape_of(dims, dtype=BF16):
    return jax.ShapeDtypeStruct(dims, dtype)


def cost(flops, moved):
    return pl.CostEstimate(flops=int(flops), bytes_accessed=int(moved), transcendentals=0)


def in_vmem():
    return pl.BlockSpec(memory_space=pltpu.VMEM)


def in_smem():
    return pl.BlockSpec(memory_space=pltpu.SMEM)


def anywhere():
    return pl.BlockSpec(memory_space=pl.ANY)


def nt_dot(left, right):
    return lax.dot_general(left, right, (((1,), (1,)), ((), ())), preferred_element_type=F32)


def edge_targets(columns, which):
    slot = lax.broadcasted_iota(jnp.int32, (2 * LAT_DEV, 1), 0)
    own = jnp.where(
        slot < LAT_DEV, slot * columns, (slot - LAT_DEV) * columns + columns - 1
    )
    if which == "own":
        return own
    row = LAT_DEV - 1 if which == "top" else 0
    shift = LAT_DEV * columns * (-1 if which == "top" else 1)
    keep = jnp.logical_or(slot == row, slot == row + LAT_DEV)
    return jnp.where(keep, own + shift, -(1 << 28))


def one_hot(targets, first, width):
    cell = lax.broadcasted_iota(jnp.int32, (1, width), 1) + first
    return jnp.where(targets == cell, 1.0, 0.0).astype(BF16)


def edges_kernel(columns, block, x_ref, out_ref, acc_ref):
    step = pl.program_id(0)

    @pl.when(step == 0)
    def _():
        acc_ref[...] = jnp.zeros_like(acc_ref)

    targets = edge_targets(columns, "own")
    total = jnp.zeros(acc_ref.shape, F32)
    for start in range(0, block, TILE):
        hot = one_hot(targets, step * block + start, TILE)
        total += nt_dot(x_ref[:, start : start + TILE], hot)
    acc_ref[...] += total

    @pl.when(step == pl.num_programs(0) - 1)
    def _():
        out_ref[...] = acc_ref[...].astype(BF16)


def block_of(cells, most):
    units = cells // TILE
    return max(k for k in range(1, units + 1) if units % k == 0 and k * TILE <= most) * TILE


def edges_of(field, columns):
    rows, cells = field.shape
    block = block_of(cells, 5120)
    return pl.pallas_call(
        functools.partial(edges_kernel, columns, block),
        grid=(cells // block,),
        in_specs=[pl.BlockSpec((rows, block), lambda i: (0, i))],
        out_specs=pl.BlockSpec((rows, 2 * LAT_DEV), lambda i: (0, 0)),
        out_shape=shape_of((rows, 2 * LAT_DEV)),
        scratch_shapes=[pltpu.VMEM((rows, 2 * LAT_DEV), F32)],
        compiler_params=params(),
        cost_estimate=cost(2 * rows * cells * 128, 2 * rows * cells),
        name="edges",
    )(field)


def lon_halo(edges):
    peers = lax.axis_size("lon")
    right = [(i, (i + 1) % peers) for i in range(peers)]
    left = [(j, i) for i, j in right]
    before = lax.ppermute(edges[:, LAT_DEV:], "lon", right)
    after = lax.ppermute(edges[:, :LAT_DEV], "lon", left)
    return jnp.concatenate([before, after], axis=1)


def lat_halo(field, cells, halo, sides):
    peers = lax.axis_size("lat")
    up = [(i, i + 1) for i in range(peers - 1)]
    down = [(j, i) for i, j in up]
    top = lax.ppermute(
        jnp.concatenate([field[:, cells - halo : cells], sides], axis=1), "lat", up
    )
    bottom = lax.ppermute(jnp.concatenate([field[:, :halo], sides], axis=1), "lat", down)
    return top, bottom


class Grid:
    def __init__(self, cells, members):
        self.cells = cells
        self.columns = cells // LAT_DEV
        self.halo = round_up(self.columns + 1, LANES)
        self.unit = members * LANES
        self.padded = round_up(cells, max(self.unit, TILE))


def window_copies(grid, first, width, field, top, bottom, target, sem):
    copies = []
    low, high = first - grid.halo, first + width + grid.halo
    for ref, begin, end in (
        (top, -grid.halo, 0),
        (field, 0, grid.cells),
        (bottom, grid.cells, grid.cells + grid.halo),
    ):
        lo, hi = max(low, begin), min(high, end)
        if lo < hi:
            copies.append(
                pltpu.make_async_copy(
                    ref.at[:, pl.ds(lo - begin, hi - lo)],
                    target.at[pl.ds(0, ref.shape[0]), pl.ds(lo - low, hi - lo)],
                    sem.at[len(copies)],
                )
            )
    return copies


def build_sides(grid, first, width, window, sides, before, after):
    total = width + 2 * grid.halo
    rows = window.shape[0]
    base = first - grid.halo
    sources = [(ref[...], edge_targets(grid.columns, which)) for ref, which in sides]
    for start in range(0, total, TILE):
        size = min(TILE, total - start)
        cell = lax.broadcasted_iota(jnp.int32, (1, size), 1) + (base + start + grid.columns)
        column = lax.rem(cell, grid.columns)
        put = jnp.zeros((rows, size), F32)
        for source, targets in sources:
            put += jnp.dot(
                source, one_hot(targets, base + start, size), preferred_element_type=F32
            )
        put = put.astype(BF16)
        lo = max(start - LANES, 0)
        hi = min(start + size + LANES, total)
        around = window[:, lo:hi]
        moved = jnp.concatenate([around[:, -1:], around[:, :-1]], axis=1)
        moved = moved[:, start - lo : start - lo + size]
        keep = jnp.where(column == 0, 0.0, 1.0).astype(BF16)
        before[:, start : start + size] = moved * keep + put * (1 - keep)
        moved = jnp.concatenate([around[:, 1:], around[:, :1]], axis=1)
        moved = moved[:, start - lo : start - lo + size]
        keep = jnp.where(column == grid.columns - 1, 0.0, 1.0).astype(BF16)
        after[:, start : start + size] = moved * keep + put * (1 - keep)


def shifted(ref, start, shift, width):
    low = shift // LANES * LANES
    off = shift - low
    if off == 0:
        return ref[:, pl.ds(start + low, width)]
    return ref[:, pl.ds(start + low, width + LANES)][:, off : off + width]


def forward_kernel(grid, first, width, has_top, has_bottom, *refs):
    refs = list(refs)
    me_ref, x_ref, sides_ref = refs[:3]
    del refs[:3]
    top_ref = refs.pop(0) if has_top else None
    bottom_ref = refs.pop(0) if has_bottom else None
    weight_ref, bias_ref = refs[:2]
    members = me_ref.shape[0]
    outs = refs[2 : 2 + members]
    window, before, after, pred, sem = refs[2 + members :]
    copies = window_copies(
        grid, first, width, x_ref, top_ref, bottom_ref, window, sem
    )
    for copy in copies:
        copy.start()
    for copy in copies:
        copy.wait()
    sources = [(sides_ref, "own")]
    if has_top:
        sources.append((top_ref.at[:, pl.ds(grid.halo, 2 * LAT_DEV)], "top"))
    if has_bottom:
        sources.append((bottom_ref.at[:, pl.ds(grid.halo, 2 * LAT_DEV)], "bottom"))
    build_sides(grid, first, width, window, sources, before, after)

    def tile(index, carry):
        start = pl.multiple_of(index * TILE, TILE)
        taps = []
        for a in range(3):
            for ref in (before, window, after):
                taps.append(shifted(ref, start, grid.halo + (a - 1) * grid.columns, TILE))
        stacked = jnp.concatenate(taps, axis=0)
        value = jnp.dot(weight_ref[...], stacked, preferred_element_type=F32)
        pred[:, pl.ds(start, TILE)] = (value + bias_ref[...]).astype(BF16)
        return carry

    lax.fori_loop(0, width // TILE, tile, 0)
    piece = width // members
    for d in range(members):
        begin = pl.multiple_of(me_ref[d] * piece, LANES)
        outs[d][...] = pred[:, pl.ds(begin, piece)]


def forward(grid, first, width, order, x, sides, top, bottom, weight, bias):
    members = order.shape[0]
    channels = x.shape[0]
    fields = weight.shape[0]
    has_top = first == 0
    has_bottom = first + width == grid.padded
    piece = width // members
    total = width + 2 * grid.halo
    operands = [order, x, sides]
    specs = [in_smem(), anywhere(), in_vmem()]
    if has_top:
        operands.append(top)
        specs.append(in_vmem())
    if has_bottom:
        operands.append(bottom)
        specs.append(in_vmem())
    operands += [weight, bias]
    specs += [in_vmem(), in_vmem()]
    return pl.pallas_call(
        functools.partial(forward_kernel, grid, first, width, has_top, has_bottom),
        in_specs=specs,
        out_specs=[in_vmem()] * members,
        out_shape=[shape_of((fields, piece))] * members,
        scratch_shapes=[
            pltpu.VMEM((channels, total), BF16),
            pltpu.VMEM((channels, total), BF16),
            pltpu.VMEM((channels, total), BF16),
            pltpu.VMEM((fields, width), BF16),
            pltpu.SemaphoreType.DMA((3,)),
        ],
        compiler_params=params(),
        cost_estimate=cost(2 * 9 * channels * 2 * fields * width, 8 * channels * width),
        name=f"forward_{first}",
    )(*operands)


def slope(values):
    return values * lax.rsqrt(values * values + 1.0)


def score_kernel(first, members, me_ref, analysis_ref, scale_ref, *refs):
    pieces = refs[:members]
    outs = refs[members : 2 * members]
    target_ref, sem = refs[2 * members :]
    piece = pieces[0].shape[1]
    begin = pl.multiple_of(first + me_ref[0] * piece, LANES)
    copy = pltpu.make_async_copy(
        analysis_ref.at[:, pl.ds(begin, piece)], target_ref, sem.at[0]
    )
    copy.start()
    copy.wait()

    def tile(index, carry):
        span = pl.ds(pl.multiple_of(index * LANES, LANES), LANES)
        values = [ref[:, span].astype(F32) for ref in pieces]
        target = target_ref[:, span].astype(F32)
        scale = scale_ref[...]
        near = scale * (1.0 / members)
        far = scale * (-1.0 / (members * (members - 1)))
        sums = [None] * members
        for i in range(members):
            for j in range(i + 1, members):
                both = slope(values[i] - values[j])
                sums[i] = both if sums[i] is None else sums[i] + both
                sums[j] = -both if sums[j] is None else sums[j] - both
        for i in range(members):
            grad = near * slope(values[i] - target) + far * sums[i]
            outs[i][:, span] = grad.astype(BF16)
        return carry

    lax.fori_loop(0, piece // LANES, tile, 0)


def score(first, order, analysis, scale, pieces):
    members = len(pieces)
    fields, piece = pieces[0].shape
    return pl.pallas_call(
        functools.partial(score_kernel, first, members),
        in_specs=[in_smem(), anywhere(), in_vmem()] + [in_vmem()] * members,
        out_specs=[in_vmem()] * members,
        out_shape=[shape_of((fields, piece))] * members,
        scratch_shapes=[pltpu.VMEM((fields, piece), BF16), pltpu.SemaphoreType.DMA((1,))],
        compiler_params=params(),
        cost_estimate=cost(100 * fields * piece * 60, 18 * fields * piece),
        name=f"score_{first}",
    )(order, analysis, scale, *pieces)


def gather_kernel(grid, first, width, members, me_ref, *refs):
    pieces = refs[:members]
    out_ref, edge_ref = refs[members:]
    fields, piece = pieces[0].shape
    pad = out_ref.shape[0] - fields
    out_ref[pl.ds(fields // 8 * 8, out_ref.shape[0] - fields // 8 * 8), :] = jnp.zeros(
        (out_ref.shape[0] - fields // 8 * 8, width), BF16
    )
    for d in range(members):
        begin = pl.multiple_of(me_ref[d] * piece, LANES)
        value = pieces[d][...]
        if grid.padded != grid.cells:
            cell = lax.broadcasted_iota(jnp.int32, (1, piece), 1) + (first + begin)
            value = jnp.where(cell < grid.cells, value.astype(F32), 0.0).astype(BF16)
        out_ref[pl.ds(0, fields), pl.ds(begin, piece)] = value
    targets = edge_targets(grid.columns, "own")

    def tile(index, total):
        start = pl.multiple_of(index * TILE, TILE)
        hot = one_hot(targets, first + start, TILE)
        return total + nt_dot(out_ref[:, pl.ds(start, TILE)], hot)

    edge_ref[...] = lax.fori_loop(
        0, width // TILE, tile, jnp.zeros(edge_ref.shape, F32)
    ).astype(BF16)


def gather(grid, first, width, rows, order, pieces):
    members = len(pieces)
    fields = pieces[0].shape[0]
    return pl.pallas_call(
        functools.partial(gather_kernel, grid, first, width, members),
        in_specs=[in_smem()] + [in_vmem()] * members,
        out_specs=[in_vmem()] * 2,
        out_shape=[shape_of((rows, width)), shape_of((rows, 2 * LAT_DEV))],
        compiler_params=params(),
        cost_estimate=cost(2 * rows * width * 128, 4 * rows * width),
        name=f"gather_{first}",
    )(order, *pieces)


def backward_kernel(grid, width, steps, x_ref, g_ref, sides_ref, top_ref, bottom_ref, weight_ref,
                    out_ref, sum_ref, window, before, after, xbuf, obuf, sem, xsem, osem):
    for number in range(steps):
        first = number * width
        copies = window_copies(grid, first, width, g_ref, top_ref, bottom_ref, window, sem)
        span = min(width, grid.cells - first)
        copies.append(
            pltpu.make_async_copy(
                x_ref.at[:, pl.ds(first, span)], xbuf.at[:, pl.ds(0, span)], xsem.at[0]
            )
        )
        for copy in copies:
            copy.start()
        for copy in copies:
            copy.wait()
        if span < width:
            xbuf[:, span:] = jnp.zeros((xbuf.shape[0], width - span), BF16)
        sources = [(sides_ref, "own")]
        if number == 0:
            sources.append((top_ref.at[:, pl.ds(grid.halo, 2 * LAT_DEV)], "top"))
        if number == steps - 1:
            sources.append((bottom_ref.at[:, pl.ds(grid.halo, 2 * LAT_DEV)], "bottom"))
        build_sides(grid, first, width, window, sources, before, after)

        def tile(index, total):
            start = pl.multiple_of(index * TILE, TILE)
            taps = []
            for a in range(3):
                for ref in (after, window, before):
                    taps.append(shifted(ref, start, grid.halo + (1 - a) * grid.columns, TILE))
            stacked = jnp.concatenate(taps, axis=0)
            value = jnp.dot(weight_ref[...], stacked, preferred_element_type=F32)
            obuf[:, pl.ds(start, TILE)] = value.astype(BF16)
            sum_ref[...] += nt_dot(xbuf[:, pl.ds(start, TILE)], stacked)
            return total + jnp.sum(
                window[:, pl.ds(grid.halo + start, TILE)].astype(F32).reshape(
                    window.shape[0], TILE), axis=1, keepdims=True)

        if number == 0:
            sum_ref[...] = jnp.zeros_like(sum_ref)
            total = jnp.zeros((window.shape[0], 1), F32)
        total = lax.fori_loop(0, width // TILE, tile, total)
        copy = pltpu.make_async_copy(
            obuf.at[:, pl.ds(0, span)], out_ref.at[:, pl.ds(first, span)], osem.at[0]
        )
        copy.start()
        copy.wait()
    return total


def backward_body(grid, width, steps, fields, *refs):
    total = backward_kernel(grid, width, steps, *refs)
    sum_ref = refs[7]
    rows = total.shape[0]
    lane = lax.broadcasted_iota(jnp.int32, (1, LANES), 1)
    sum_ref[pl.ds(0, rows), :LANES] = jnp.where(
        lane == fields, total, sum_ref[pl.ds(0, rows), :LANES]
    )


def backward(grid, x, g, sides, top, bottom, weight, fields):
    channels = x.shape[0]
    rows = g.shape[0]
    width = block_of(grid.padded, 5120)
    steps = grid.padded // width
    total = width + 2 * grid.halo
    return pl.pallas_call(
        functools.partial(backward_body, grid, width, steps, fields),
        in_specs=[anywhere(), anywhere()] + [in_vmem()] * 4,
        out_specs=[anywhere(), in_vmem()],
        out_shape=[shape_of((channels, grid.cells)), shape_of((channels, 9 * rows), F32)],
        scratch_shapes=[
            pltpu.VMEM((rows, total), BF16),
            pltpu.VMEM((rows, total), BF16),
            pltpu.VMEM((rows, total), BF16),
            pltpu.VMEM((channels, width), BF16),
            pltpu.VMEM((channels, width), BF16),
            pltpu.SemaphoreType.DMA((3,)),
            pltpu.SemaphoreType.DMA((1,)),
            pltpu.SemaphoreType.DMA((1,)),
        ],
        compiler_params=params(),
        cost_estimate=cost(4 * 9 * channels * rows * grid.cells, 8 * channels * grid.cells),
        name="backward",
    )(x, g, sides, top, bottom, weight)


def sum_all(value):
    halved = []
    for axis in ("lat", "member", "lon"):
        bit = 1
        while bit < lax.axis_size(axis):
            swap = [(i, i ^ bit) for i in range(lax.axis_size(axis))]
            rows = value.shape[0]
            if rows % 16 == 0 and len(halved) < 2:
                upper = (lax.axis_index(axis) & bit) != 0
                low, high = value[: rows // 2], value[rows // 2 :]
                keep, send = (jnp.where(upper, high, low), jnp.where(upper, low, high))
                value = keep + lax.ppermute(send, axis, swap)
                halved.append((axis, swap, upper))
            else:
                value = value + lax.ppermute(value, axis, swap)
            bit *= 2
    for axis, swap, upper in reversed(halved):
        other = lax.ppermute(value, axis, swap)
        value = jnp.where(
            upper,
            jnp.concatenate([other, value], axis=0),
            jnp.concatenate([value, other], axis=0),
        )
    return value


def chunks_of(grid):
    units = grid.padded // TILE
    count = 5 if units % 5 == 0 else (3 if units % 3 == 0 else 1)
    width = units // count * TILE
    return [(i * width, width) for i in range(count)]


def local(inputs, weight, bias, analysis, field_weight):
    channels, cells = inputs.shape[1], inputs.shape[4]
    fields = analysis.shape[0]
    members = lax.axis_size("member")
    grid = Grid(cells, members)
    x = inputs.reshape(channels, cells)
    target = analysis.reshape(fields, cells)
    if grid.padded != cells:
        x_wide = jnp.pad(x, ((0, 0), (0, grid.padded - cells)))
        target = jnp.pad(target, ((0, 0), (0, grid.padded - cells)))
    else:
        x_wide = x
    rows = round_up(fields, 16)
    taps = weight.reshape(9, channels, fields)
    forward_weight = taps.transpose(2, 0, 1).reshape(fields, 9 * channels)
    backward_weight = jnp.pad(taps, ((0, 0), (0, 0), (0, rows - fields)))
    backward_weight = backward_weight.transpose(1, 0, 2).reshape(channels, 9 * rows)
    me = lax.axis_index("member").astype(jnp.int32)
    order = me ^ jnp.arange(members, dtype=jnp.int32)
    scale = field_weight[:, None]
    shift = bias[:, None]

    x_sides = lon_halo(edges_of(x_wide, grid.columns))
    x_top, x_bottom = lat_halo(x, cells, grid.halo, x_sides)

    def to_members(pieces):
        moved = [pieces[0]]
        for d in range(1, members):
            moved.append(lax.ppermute(pieces[d], "member", [(i, i ^ d) for i in range(members)]))
        return moved

    chunks = chunks_of(grid)
    received = []
    for first, width in chunks:
        pieces = forward(
            grid, first, width, order, x, x_sides, x_top, x_bottom, forward_weight, shift
        )
        received.append(to_members(pieces))
    returned = []
    for (first, width), pieces in zip(chunks, received):
        returned.append(to_members(score(first, order, target, scale, pieces)))
    parts, edges = [], []
    for (first, width), pieces in zip(chunks, returned):
        part, edge = gather(grid, first, width, rows, order, pieces)
        parts.append(part)
        edges.append(edge)
    g = jnp.concatenate(parts, axis=1)
    g_edges = sum(edges[1:], edges[0])
    g_sides = lon_halo(g_edges)
    g_top, g_bottom = lat_halo(g, cells, grid.halo, g_sides)
    grad_input, sums = backward(grid, x, g, g_sides, g_top, g_bottom, backward_weight, fields)
    total = sum_all(sums) / (cells * lax.axis_size("lat") * lax.axis_size("lon"))
    by_tap = total.reshape(channels, 9, rows)[:, :, :fields].transpose(1, 0, 2)
    grad_weight = by_tap.reshape(9, channels * fields)
    grad_bias = total[:fields, fields]
    return (grad_input.reshape(1, channels, 1, 1, cells), grad_weight, grad_bias)


def solution(mesh):
    placed = (P("member", None, "lat", "lon", None), P(), P(), P(None, "lat", "lon", None), P())
    return jax.shard_map(
        local,
        mesh=mesh,
        in_specs=placed,
        out_specs=(P("member", None, "lat", "lon", None), P(), P()),
        check_vma=False,
    )
```

time: 605 us -> 271 us (0.45); the launches traced: 594 us -> 270 us
  local copies, waits for them, and re-layouts: 273 us -> 17.2 us
  Pallas kernels: 0 us -> 158 us
  matrix products: 94.8 us -> 0 us
  blocking collectives: 87.5 us -> 0 us
  other arithmetic: 65.1 us -> 5.93 us
  starting transfers between devices: 21.9 us -> 55.3 us
  between operations: 15.5 us -> 1.35 us
    pallas_call x0 -> x17, Pallas kernels: none -> 158 us  [the longest x1 59.6 us: backward(): pl.pallas_call(functools.partial(backward_body, grid, width, steps, field...]
    reshape x17 -> x4, local copies, waits for them, and re-layouts: 154 us -> 3.61 us  [the longest x1 1.18 us: local(): grad_weight = by_tap.reshape(9, channels * fields)]
    dot_general x27 -> x0, matrix products: 94.8 us -> none  [the longest x9 41.8 us: local(): jnp.dot(tap_weights[tap_index].T, window, preferred_element_type=jnp.floa...]
    another operation x5 -> x0, local copies, waits for them, and re-layouts: 54.7 us -> none  [the longest x2 19.5 us: local(): prediction[None]]
    all_to_all x1 -> x0, blocking collectives: 50.6 us -> none  [local(): lax.all_to_all(cell_grad, 'member', split_axis=0, concat_axis=2, tiled=True)]
    concatenate x5 -> x4, other arithmetic: 44.7 us -> 1.54 us  [the longest x2 1.37 us: lon_halo(): return jnp.concatenate([before, after], axis=1)]
    ppermute x8 -> x45, starting transfers between devices: 17 us -> 55.3 us  [the longest x30 35.7 us: to_members(): lax.ppermute(pieces[d], 'member', [(i, i ^ d) for i in range(members)])]
    slice x10 -> x5, local copies, waits for them, and re-layouts: 40.5 us -> 2.8 us  [the longest x2 1.83 us: lat_halo(): field[:, :halo]]
  transfers between devices with their start and end apart: 10 -> 45, of which waited for: 1 -> 14; matrix products, arithmetic and copies ran while one was open for 34% -> 5% of each run, Pallas kernels for 0% -> 33%
where the time goes in v1:
time: 271 us; the launch traced here: 270 us
  Pallas kernels  158 us (58%)
  starting transfers between devices  55.3 us (20%)
  waiting for transfers between devices  31.8 us (12%)
  local copies, waits for them, and re-layouts  17.2 us (6%)
  other arithmetic  5.93 us (2%)
    pallas_call x1, Pallas kernels, backward(): pl.pallas_call(functools.partial(backward_body, grid, width, steps, field...  59.6 us
    pallas_call x5, Pallas kernels, forward(): pl.pallas_call(functools.partial(forward_kernel, grid, first, width, has_...  52.4 us
    ppermute x30, starting transfers between devices, to_members(): lax.ppermute(pieces[d], 'member', [(i, i ^ d) for i in range(members)])  35.7 us
    pallas_call x5, Pallas kernels, score(): pl.pallas_call(functools.partial(score_kernel, first, members), in_specs=...  21.7 us
    pallas_call x5, Pallas kernels, gather(): pl.pallas_call(functools.partial(gather_kernel, grid, first, width, membe...  18.9 us
    ppermute x3, waiting for transfers between devices, sum_all(): value = value + lax.ppermute(value, axis, swap)  12.7 us
    unnamed x114, local copies, waits for them, and re-layouts  7.66 us
    ppermute x30, waiting for transfers between devices, to_members(): lax.ppermute(pieces[d], 'member', [(i, i ^ d) for i in range(members)])  7.28 us
  transfers between devices with their start and end apart: 45, of which 14 were waited for; matrix products, arithmetic and copies ran while one was open for 5% of the time, Pallas kernels for 33%

profile of v1, /device:TPU:0, one launch (start us, length us, event | category | flops | bytes accessed | tf_op | source)
XLA Modules:
  0.0 270.0 jit_solution(13553788494583176437)
XLA Ops:
  0.7 5.8 %edges.1 = bf16[96,128]{1,0:T(8,128)(2,1)} custom-call(bf16[96,23040]{1,0:T(8,128)(2,1)} %bitcast.18), custom_call_target="tpu_custom_call" | custom-call | flops 566231040 | bytes 4423680 | tf_op jit(solution)/shard_map/edges/pallas_call | solution.py:95
  7.3 5.1 %collective-permute-start.1 = (bf16[96,64]{1,0:T(8,128)(2,1)S(1)}, bf16[96,64]{1,0:T(8,128)(2,1)S(1)}, u32[]{:S(2)}, u32[]{:S(2)}) collective-permute-start(bf16[96,64]{1,0:T(8,128)(2,1)S(1)} %get-tuple-element.116), channel_id=1, source_target_pairs={{1,0},{2,1},{3,2},{0,3},{5,4},{6,5},{7,6},{4,7},{9,8},{10,9},{11,1... | collective-permute-start | bytes 36872 | tf_op jit(solution)/shard_map/ppermute | solution.py:113
  16.2 1.8 collective-permute-done
  18.1 1.3 collective-permute-start.2
  20.1 10.4 %forward_4608.1 = (bf16[84,1152]{1,0:T(8,128)(2,1)}, bf16[84,1152]{1,0:T(8,128)(2,1)}, bf16[84,1152]{1,0:T(8,128)(2,1)}, bf16[84,1152]{1,0:T(8,128)(2,1)}) custom-call(s32[4]{0:T(128)} %iota_xor_fusion.refs_0_.me_ref, bf16[96,23040]{1,0:T(8,128)(2,1)} %bitcast.20, bf16[96,128]{1,0:T(8,128)(2,1)} %pad_maximum_fusion.12.refs_2_, ...), custom_call_target="tpu_custom_call" | custom-call | flops 1337720832 | bytes 3538944 | tf_op jit(solution)/shard_map/forward_4608/pallas_call | solution.py:253
  30.5 1.6 collective-permute-start.9
  32.1 1.5 collective-permute-start.10
  33.6 1.6 collective-permute-start.27
  35.2 10.5 %forward_9216.1 = (bf16[84,1152]{1,0:T(8,128)(2,1)}, bf16[84,1152]{1,0:T(8,128)(2,1)}, bf16[84,1152]{1,0:T(8,128)(2,1)}, bf16[84,1152]{1,0:T(8,128)(2,1)}) custom-call(s32[4]{0:T(128)} %iota_xor_fusion.refs_0_.me_ref, bf16[96,23040]{1,0:T(8,128)(2,1)} %bitcast.21, bf16[96,128]{1,0:T(8,128)(2,1)} %pad_maximum_fusion.12.refs_2_, ...), custom_call_target="tpu_custom_call" | custom-call | flops 1337720832 | bytes 3538944 | tf_op jit(solution)/shard_map/forward_9216/pallas_call | solution.py:253
  45.7 10.5 %forward_13824.1 = (bf16[84,1152]{1,0:T(8,128)(2,1)}, bf16[84,1152]{1,0:T(8,128)(2,1)}, bf16[84,1152]{1,0:T(8,128)(2,1)}, bf16[84,1152]{1,0:T(8,128)(2,1)}) custom-call(s32[4]{0:T(128)} %iota_xor_fusion.refs_0_.me_ref, bf16[96,23040]{1,0:T(8,128)(2,1)} %bitcast.22, bf16[96,128]{1,0:T(8,128)(2,1)} %pad_maximum_fusion.12.refs_2_, ...), custom_call_target="tpu_custom_call" | custom-call | flops 1337720832 | bytes 3538944 | tf_op jit(solution)/shard_map/forward_13824/pallas_call | solution.py:253
  56.8 1.6 collective-permute-start.15
  58.4 1.6 collective-permute-start.16
  60.5 1.5 collective-permute-start.21
  62.0 10.5 %forward_0.1 = (bf16[84,1152]{1,0:T(8,128)(2,1)}, bf16[84,1152]{1,0:T(8,128)(2,1)}, bf16[84,1152]{1,0:T(8,128)(2,1)}, bf16[84,1152]{1,0:T(8,128)(2,1)}) custom-call(s32[4]{0:T(128)} %iota_xor_fusion.refs_0_.me_ref, bf16[96,23040]{1,0:T(8,128)(2,1)} %bitcast.23, bf16[96,128]{1,0:T(8,128)(2,1)} %pad_maximum_fusion.12.refs_2_, bf16[96,512]{1,0:T(8,128)(2,1)} %copy-done.52, ...), custom_call_target="tpu_custom_call" | custom-call | flops 1337720832 | bytes 3538944 | tf_op jit(solution)/shard_map/forward_0/pallas_call | solution.py:253
  72.5 1.6 collective-permute-start.22
  74.6 1.5 collective-permute-start.3
  76.1 1.5 collective-permute-start.4
  79.3 10.5 %forward_18432.1 = (bf16[84,1152]{1,0:T(8,128)(2,1)}, bf16[84,1152]{1,0:T(8,128)(2,1)}, bf16[84,1152]{1,0:T(8,128)(2,1)}, bf16[84,1152]{1,0:T(8,128)(2,1)}) custom-call(s32[4]{0:T(128)} %iota_xor_fusion.refs_0_.me_ref, bf16[96,23040]{1,0:T(8,128)(2,1)} %bitcast.24, bf16[96,128]{1,0:T(8,128)(2,1)} %pad_maximum_fusion.12.refs_2_, bf16[96,512]{1,0:T(8,128)(2,1)} %copy-done.51, ...), custom_call_target="tpu_custom_call" | custom-call | flops 1337720832 | bytes 3538944 | tf_op jit(solution)/shard_map/forward_18432/pallas_call | solution.py:253
  89.9 4.4 %score_4608.1 = (bf16[84,1152]{1,0:T(8,128)(2,1)}, bf16[84,1152]{1,0:T(8,128)(2,1)}, bf16[84,1152]{1,0:T(8,128)(2,1)}, bf16[84,1152]{1,0:T(8,128)(2,1)}) custom-call(s32[4]{0:T(128)} %iota_xor_fusion.refs_0_.me_ref, bf16[84,23040]{1,0:T(8,128)(2,1)} %bitcast.13, f32[84,1]{1,0:T(8,128)} %copy.23.scale_ref, bf16[84,1152]{1,0:T(8,128)(2,1)} %get-tuple-element.64.refs_0_, ...), custom_call_target="tpu_custom_call" | custom-call | flops 580608000 | bytes 1741824 | tf_op jit(solution)/shard_map/score_4608/pallas_call | solution.py:311
  94.4 1.6 collective-permute-start.28
  98.1 1.5 collective-permute-start.12
  100.7 4.3 %score_9216.1 = (bf16[84,1152]{1,0:T(8,128)(2,1)}, bf16[84,1152]{1,0:T(8,128)(2,1)}, bf16[84,1152]{1,0:T(8,128)(2,1)}, bf16[84,1152]{1,0:T(8,128)(2,1)}) custom-call(s32[4]{0:T(128)} %iota_xor_fusion.refs_0_.me_ref, bf16[84,23040]{1,0:T(8,128)(2,1)} %bitcast.14, f32[84,1]{1,0:T(8,128)} %copy.23.scale_ref, bf16[84,1152]{1,0:T(8,128)(2,1)} %get-tuple-element.73.refs_0_, ...), custom_call_target="tpu_custom_call" | custom-call | flops 580608000 | bytes 1741824 | tf_op jit(solution)/shard_map/score_9216/pallas_call | solution.py:311
  105.1 4.4 %score_13824.1 = (bf16[84,1152]{1,0:T(8,128)(2,1)}, bf16[84,1152]{1,0:T(8,128)(2,1)}, bf16[84,1152]{1,0:T(8,128)(2,1)}, bf16[84,1152]{1,0:T(8,128)(2,1)}) custom-call(s32[4]{0:T(128)} %iota_xor_fusion.refs_0_.me_ref, bf16[84,23040]{1,0:T(8,128)(2,1)} %bitcast.15, f32[84,1]{1,0:T(8,128)} %copy.23.scale_ref, bf16[84,1152]{1,0:T(8,128)(2,1)} %get-tuple-element.82.refs_0_, ...), custom_call_target="tpu_custom_call" | custom-call | flops 580608000 | bytes 1741824 | tf_op jit(solution)/shard_map/score_13824/pallas_call | solution.py:311
  110.5 1.6 collective-permute-start.18
  114.2 1.5 collective-permute-start.24
  115.7 4.4 %score_0.1 = (bf16[84,1152]{1,0:T(8,128)(2,1)}, bf16[84,1152]{1,0:T(8,128)(2,1)}, bf16[84,1152]{1,0:T(8,128)(2,1)}, bf16[84,1152]{1,0:T(8,128)(2,1)}) custom-call(s32[4]{0:T(128)} %iota_xor_fusion.refs_0_.me_ref, bf16[84,23040]{1,0:T(8,128)(2,1)} %bitcast.16, f32[84,1]{1,0:T(8,128)} %copy.23.scale_ref, bf16[84,1152]{1,0:T(8,128)(2,1)} %get-tuple-element.55.refs_0_, ...), custom_call_target="tpu_custom_call" | custom-call | flops 580608000 | bytes 1741824 | tf_op jit(solution)/shard_map/score_0/pallas_call | solution.py:311
  125.0 2.3 collective-permute-done.20.refs_3_
  128.2 2.8 %collective-permute-done.24.refs_1_ = bf16[84,1152]{1,0:T(8,128)(2,1)S(1)} collective-permute-done((bf16[84,1152]{1,0:T(8,128)(2,1)}, bf16[84,1152]{1,0:T(8,128)(2,1)S(1)}, u32[]{:S(2)}, u32[]{:S(2)}) %collective-permute-start.24) | collective-permute-done | bytes 193568 | tf_op jit(solution)/shard_map/ppermute | solution.py:512
  133.2 4.3 %score_18432.1 = (bf16[84,1152]{1,0:T(8,128)(2,1)}, bf16[84,1152]{1,0:T(8,128)(2,1)}, bf16[84,1152]{1,0:T(8,128)(2,1)}, bf16[84,1152]{1,0:T(8,128)(2,1)}) custom-call(s32[4]{0:T(128)} %iota_xor_fusion.refs_0_.me_ref, bf16[84,23040]{1,0:T(8,128)(2,1)} %bitcast.17, f32[84,1]{1,0:T(8,128)} %copy.23.scale_ref, bf16[84,1152]{1,0:T(8,128)(2,1)} %get-tuple-element.91.refs_0_, ...), custom_call_target="tpu_custom_call" | custom-call | flops 580608000 | bytes 1741824 | tf_op jit(solution)/shard_map/score_18432/pallas_call | solution.py:311
  137.5 3.8 %gather_4608.1 = (bf16[96,4608]{1,0:T(8,128)(2,1)}, bf16[96,128]{1,0:T(8,128)(2,1)}) custom-call(s32[4]{0:T(128)} %iota_xor_fusion.refs_0_.me_ref, bf16[84,1152]{1,0:T(8,128)(2,1)} %get-tuple-element.68.refs_0_, bf16[84,1152]{1,0:T(8,128)(2,1)} %copy-done.20, bf16[84,1152]{1,0:T(8,128)(2,1)} %copy-done.21, bf16[84,1152]{1,0:T(8,128)(2,1)} %copy-done.22), custom_call_target="tpu_custom_call" | custom-call | flops 113246208 | bytes 1769472 | tf_op jit(solution)/shard_map/gather_4608/pallas_call | solution.py:353
  141.3 3.8 %gather_9216.1 = (bf16[96,4608]{1,0:T(8,128)(2,1)}, bf16[96,128]{1,0:T(8,128)(2,1)}) custom-call(s32[4]{0:T(128)} %iota_xor_fusion.refs_0_.me_ref, bf16[84,1152]{1,0:T(8,128)(2,1)} %get-tuple-element.77.refs_0_, bf16[84,1152]{1,0:T(8,128)(2,1)} %copy-done.23, bf16[84,1152]{1,0:T(8,128)(2,1)} %copy-done.25, bf16[84,1152]{1,0:T(8,128)(2,1)} %copy-done.27), custom_call_target="tpu_custom_call" | custom-call | flops 113246208 | bytes 1769472 | tf_op jit(solution)/shard_map/gather_9216/pallas_call | solution.py:353
  145.1 1.6 collective-permute-start.31
  147.5 3.8 %gather_13824.1 = (bf16[96,4608]{1,0:T(8,128)(2,1)}, bf16[96,128]{1,0:T(8,128)(2,1)}) custom-call(s32[4]{0:T(128)} %iota_xor_fusion.refs_0_.me_ref, bf16[84,1152]{1,0:T(8,128)(2,1)} %get-tuple-element.86.refs_0_, bf16[84,1152]{1,0:T(8,128)(2,1)} %copy-done.24, bf16[84,1152]{1,0:T(8,128)(2,1)} %copy-done.28, bf16[84,1152]{1,0:T(8,128)(2,1)} %copy-done.30), custom_call_target="tpu_custom_call" | custom-call | flops 113246208 | bytes 1769472 | tf_op jit(solution)/shard_map/gather_13824/pallas_call | solution.py:353
  153.3 3.7 %gather_0.1 = (bf16[96,4608]{1,0:T(8,128)(2,1)}, bf16[96,128]{1,0:T(8,128)(2,1)}) custom-call(s32[4]{0:T(128)} %iota_xor_fusion.refs_0_.me_ref, bf16[84,1152]{1,0:T(8,128)(2,1)} %get-tuple-element.59.refs_0_, bf16[84,1152]{1,0:T(8,128)(2,1)} %copy-done.26, bf16[84,1152]{1,0:T(8,128)(2,1)} %copy-done.29, bf16[84,1152]{1,0:T(8,128)(2,1)} %copy-done.31), custom_call_target="tpu_custom_call" | custom-call | flops 113246208 | bytes 1769472 | tf_op jit(solution)/shard_map/gather_0/pallas_call | solution.py:353
  157.0 2.2 constant_dynamic-update-slice_fusion.4
  160.1 3.8 %gather_18432.1 = (bf16[96,4608]{1,0:T(8,128)(2,1)}, bf16[96,128]{1,0:T(8,128)(2,1)}) custom-call(s32[4]{0:T(128)} %iota_xor_fusion.refs_0_.me_ref, bf16[84,1152]{1,0:T(8,128)(2,1)} %get-tuple-element.95.refs_0_, bf16[84,1152]{1,0:T(8,128)(2,1)} %copy-done.32, bf16[84,1152]{1,0:T(8,128)(2,1)} %copy-done.33, bf16[84,1152]{1,0:T(8,128)(2,1)} %copy-done.34), custom_call_target="tpu_custom_call" | custom-call | flops 113246208 | bytes 1769472 | tf_op jit(solution)/shard_map/gather_18432/pallas_call | solution.py:353
  164.8 2.0 collective-permute-start.35
  172.5 1.3 collective-permute-start.36
  173.8 1.5 collective-permute-start.37
  177.7 59.6 %backward.1 = (bf16[96,23040]{1,0:T(8,128)(2,1)}, f32[96,864]{1,0:T(8,128)}) custom-call(bf16[96,23040]{1,0:T(8,128)(2,1)} %bitcast.25, bf16[96,23040]{1,0:T(8,128)(2,1)} %constant_dynamic-update-slice_fusion.refs_1_, bf16[96,128]{1,0:T(8,128)(2,1)} %pad_maximum_fusion.13.refs_2_, bf16[96,512]{1,0:T(8,128)(2,1)} %copy-done.53, bf16[96,512]{1,0:T(8,128)(2,1)} %copy-done.54, ...), custom_call_target="tpu_custom_call" | custom-call | flops 7644119040 | bytes 17694720 | tf_op jit(solution)/shard_map/backward/pallas_call | solution.py:430
  241.3 1.6 collective-permute-start.39
  242.9 3.3 %collective-permute-done.39 = f32[24,864]{1,0:T(8,128)S(1)} collective-permute-done((f32[24,864]{1,0:T(8,128)S(1)}, f32[24,864]{1,0:T(8,128)S(1)}, u32[]{:S(2)}, u32[]{:S(2)}) %collective-permute-start.39) | collective-permute-done | bytes 82976 | tf_op jit(solution)/shard_map/ppermute | solution.py:462
  247.1 3.6 %collective-permute-done.40 = f32[24,864]{1,0:T(8,128)S(1)} collective-permute-done((f32[24,864]{1,0:T(8,128)S(1)}, f32[24,864]{1,0:T(8,128)S(1)}, u32[]{:S(2)}, u32[]{:S(2)}) %collective-permute-start.40) | collective-permute-done | bytes 82976 | tf_op jit(solution)/shard_map/ppermute | solution.py:465
  250.8 4.5 %collective-permute-done.41 = f32[24,864]{1,0:T(8,128)S(1)} collective-permute-done((f32[24,864]{1,0:T(8,128)S(1)}, f32[24,864]{1,0:T(8,128)S(1)}, u32[]{:S(2)}, u32[]{:S(2)}) %collective-permute-start.41) | collective-permute-done | bytes 82976 | tf_op jit(solution)/shard_map/ppermute | solution.py:465
  255.3 1.8 collective-permute-start.42
  257.1 4.5 %collective-permute-done.42 = f32[24,864]{1,0:T(8,128)S(1)} collective-permute-done((f32[24,864]{1,0:T(8,128)S(1)}, f32[24,864]{1,0:T(8,128)S(1)}, u32[]{:S(2)}, u32[]{:S(2)}) %collective-permute-start.42) | collective-permute-done | bytes 82976 | tf_op jit(solution)/shard_map/ppermute | solution.py:465
  261.7 1.6 collective-permute-start.43
  263.3 3.0 %collective-permute-done.43 = f32[24,864]{1,0:T(8,128)S(1)} collective-permute-done((f32[24,864]{1,0:T(8,128)S(1)}, f32[24,864]{1,0:T(8,128)S(1)}, u32[]{:S(2)}, u32[]{:S(2)}) %collective-permute-start.43) | collective-permute-done | bytes 82976 | tf_op jit(solution)/shard_map/ppermute | solution.py:468
  (208 shorter events, 44.5 us)
Async XLA Ops:
  7.3 8.9 %collective-permute-start.1 = (bf16[96,64]{1,0:T(8,128)(2,1)S(1)}, bf16[96,64]{1,0:T(8,128)(2,1)S(1)}, u32[]{:S(2)}, u32[]{:S(2)}) collective-permute-start(bf16[96,64]{1,0:T(8,128)(2,1)S(1)} %get-tuple-element.116), channel_id=1, source_target_pairs={{1,0},{2,1},{3,2},{0,3},{5,4},{6,5},{7,6},{4,7},{9,8},{10,9},{11,1... | collective-permute-start | bytes 36872 | tf_op jit(solution)/shard_map/ppermute | solution.py:113
  12.4 5.6 %collective-permute-start = (bf16[96,64]{1,0:T(8,128)(2,1)S(1)}, bf16[96,64]{1,0:T(8,128)(2,1)S(1)}, u32[]{:S(2)}, u32[]{:S(2)}) collective-permute-start(bf16[96,64]{1,0:T(8,128)(2,1)S(1)} %get-tuple-element.115), channel_id=1, source_target_pairs={{0,1},{1,2},{2,3},{3,0},{4,5},{5,6},{6,7},{7,4},{8,9},{9,10},{10,1... | collective-permute-start | bytes 36872 | tf_op jit(solution)/shard_map/ppermute | solution.py:112
  18.1 38.7 %collective-permute-start.2 = (bf16[96,512]{1,0:T(8,128)(2,1)S(1)}, bf16[96,512]{1,0:T(8,128)(2,1)S(1)}, u32[]{:S(2)}, u32[]{:S(2)}) collective-permute-start(bf16[96,512]{1,0:T(8,128)(2,1)S(1)} %get-tuple-element.112), channel_id=1, source_target_pairs={{0,4},{1,5},{2,6},{3,7},{8,12},{9,13},{10,14},{11,15},{16,20},{17,... | collective-permute-start | bytes 294920 | tf_op jit(solution)/shard_map/ppermute | solution.py:121
  30.5 29.5 %collective-permute-start.9 = (bf16[84,1152]{1,0:T(8,128)(2,1)}, bf16[84,1152]{1,0:T(8,128)(2,1)S(1)}, u32[]{:S(2)}, u32[]{:S(2)}) collective-permute-start(bf16[84,1152]{1,0:T(8,128)(2,1)} %get-tuple-element.65), channel_id=1, source_target_pairs={{0,8},{8,0},{16,24},{24,16},{1,9},{9,1},{17,25},{25,17},{2,10},{10... | collective-permute-start | bytes 580616 | tf_op jit(solution)/shard_map/ppermute | solution.py:512
  32.1 28.4 %collective-permute-start.10 = (bf16[84,1152]{1,0:T(8,128)(2,1)}, bf16[84,1152]{1,0:T(8,128)(2,1)S(1)}, u32[]{:S(2)}, u32[]{:S(2)}) collective-permute-start(bf16[84,1152]{1,0:T(8,128)(2,1)} %get-tuple-element.66), channel_id=1, source_target_pairs={{0,16},{8,24},{16,0},{24,8},{1,17},{9,25},{17,1},{25,9},{2,18},{10... | collective-permute-start | bytes 580616 | tf_op jit(solution)/shard_map/ppermute | solution.py:512
  33.6 24.8 %collective-permute-start.27 = (bf16[96,512]{1,0:T(8,128)(2,1)S(1)}, bf16[96,512]{1,0:T(8,128)(2,1)S(1)}, u32[]{:S(2)}, u32[]{:S(2)}) collective-permute-start(bf16[96,512]{1,0:T(8,128)(2,1)S(1)} %get-tuple-element.111), channel_id=1, source_target_pairs={{4,0},{5,1},{6,2},{7,3},{12,8},{13,9},{14,10},{15,11},{20,16},{21,... | collective-permute-start | bytes 294920 | tf_op jit(solution)/shard_map/ppermute | solution.py:124
  45.7 32.9 %copy-start.37 = (f32[84]{0:T(128)S(1)}, f32[84]{0:T(128)}, u32[]{:S(2)}) copy-start(f32[84]{0:T(128)} %param.9) | copy-start | bytes 1012
  56.3 16.2 %collective-permute-start.11 = (bf16[84,1152]{1,0:T(8,128)(2,1)S(1)}, bf16[84,1152]{1,0:T(8,128)(2,1)S(1)}, u32[]{:S(2)}, u32[]{:S(2)}) collective-permute-start(bf16[84,1152]{1,0:T(8,128)(2,1)S(1)} %copy-done.48), channel_id=1, source_target_pairs={{0,24},{8,16},{16,8},{24,0},{1,25},{9,17},{17,9},{25,1},{2,26},{10... | collective-permute-start | bytes 580616 | tf_op jit(solution)/shard_map/ppermute | solution.py:512
  56.8 17.3 %collective-permute-start.15 = (bf16[84,1152]{1,0:T(8,128)(2,1)S(1)}, bf16[84,1152]{1,0:T(8,128)(2,1)S(1)}, u32[]{:S(2)}, u32[]{:S(2)}) collective-permute-start(bf16[84,1152]{1,0:T(8,128)(2,1)S(1)} %copy-done.50), channel_id=1, source_target_pairs={{0,8},{8,0},{16,24},{24,16},{1,9},{9,1},{17,25},{25,17},{2,10},{10... | collective-permute-start | bytes 580616 | tf_op jit(solution)/shard_map/ppermute | solution.py:512
  58.4 16.3 %collective-permute-start.16 = (bf16[84,1152]{1,0:T(8,128)(2,1)S(1)}, bf16[84,1152]{1,0:T(8,128)(2,1)S(1)}, u32[]{:S(2)}, u32[]{:S(2)}) collective-permute-start(bf16[84,1152]{1,0:T(8,128)(2,1)S(1)} %copy-done.49), channel_id=1, source_target_pairs={{0,16},{8,24},{16,0},{24,8},{1,17},{9,25},{17,1},{25,9},{2,18},{10... | collective-permute-start | bytes 580616 | tf_op jit(solution)/shard_map/ppermute | solution.py:512
  60.0 29.9 %copy-start.15 = (bf16[84,1152]{1,0:T(8,128)(2,1)}, bf16[84,1152]{1,0:T(8,128)(2,1)S(1)}, u32[]{:S(2)}) copy-start(bf16[84,1152]{1,0:T(8,128)(2,1)S(1)} %collective-permute-done.9.refs_1_) | copy-start | bytes 580612
  60.0 16.2 %collective-permute-start.17 = (bf16[84,1152]{1,0:T(8,128)(2,1)S(1)}, bf16[84,1152]{1,0:T(8,128)(2,1)S(1)}, u32[]{:S(2)}, u32[]{:S(2)}) collective-permute-start(bf16[84,1152]{1,0:T(8,128)(2,1)S(1)} %copy-done.47), channel_id=1, source_target_pairs={{0,24},{8,16},{16,8},{24,0},{1,25},{9,17},{17,9},{25,1},{2,26},{10... | collective-permute-start | bytes 580616 | tf_op jit(solution)/shard_map/ppermute | solution.py:512
  60.5 29.4 %copy-start.16 = (bf16[84,1152]{1,0:T(8,128)(2,1)}, bf16[84,1152]{1,0:T(8,128)(2,1)S(1)}, u32[]{:S(2)}) copy-start(bf16[84,1152]{1,0:T(8,128)(2,1)S(1)} %collective-permute-done.10.refs_2_) | copy-start | bytes 580612
  60.5 17.2 %collective-permute-start.21 = (bf16[84,1152]{1,0:T(8,128)(2,1)}, bf16[84,1152]{1,0:T(8,128)(2,1)S(1)}, u32[]{:S(2)}, u32[]{:S(2)}) collective-permute-start(bf16[84,1152]{1,0:T(8,128)(2,1)} %get-tuple-element.83), channel_id=1, source_target_pairs={{0,8},{8,0},{16,24},{24,16},{1,9},{9,1},{17,25},{25,17},{2,10},{10... | collective-permute-start | bytes 580616 | tf_op jit(solution)/shard_map/ppermute | solution.py:512
  72.5 21.8 %collective-permute-start.22 = (bf16[84,1152]{1,0:T(8,128)(2,1)S(1)}, bf16[84,1152]{1,0:T(8,128)(2,1)S(1)}, u32[]{:S(2)}, u32[]{:S(2)}) collective-permute-start(bf16[84,1152]{1,0:T(8,128)(2,1)S(1)} %copy-done.40), channel_id=1, source_target_pairs={{0,16},{8,24},{16,0},{24,8},{1,17},{9,25},{17,1},{25,9},{2,18},{10... | collective-permute-start | bytes 580616 | tf_op jit(solution)/shard_map/ppermute | solution.py:512
  74.1 21.8 %collective-permute-start.23 = (bf16[84,1152]{1,0:T(8,128)(2,1)S(1)}, bf16[84,1152]{1,0:T(8,128)(2,1)S(1)}, u32[]{:S(2)}, u32[]{:S(2)}) collective-permute-start(bf16[84,1152]{1,0:T(8,128)(2,1)S(1)} %copy-done.39), channel_id=1, source_target_pairs={{0,24},{8,16},{16,8},{24,0},{1,25},{9,17},{17,9},{25,1},{2,26},{10... | collective-permute-start | bytes 580616 | tf_op jit(solution)/shard_map/ppermute | solution.py:512
  74.6 22.5 %collective-permute-start.3 = (bf16[84,1152]{1,0:T(8,128)(2,1)}, bf16[84,1152]{1,0:T(8,128)(2,1)S(1)}, u32[]{:S(2)}, u32[]{:S(2)}) collective-permute-start(bf16[84,1152]{1,0:T(8,128)(2,1)} %get-tuple-element.56), channel_id=1, source_target_pairs={{0,8},{8,0},{16,24},{24,16},{1,9},{9,1},{17,25},{25,17},{2,10},{10... | collective-permute-start | bytes 580616 | tf_op jit(solution)/shard_map/ppermute | solution.py:512
  76.1 21.9 %collective-permute-start.4 = (bf16[84,1152]{1,0:T(8,128)(2,1)}, bf16[84,1152]{1,0:T(8,128)(2,1)S(1)}, u32[]{:S(2)}, u32[]{:S(2)}) collective-permute-start(bf16[84,1152]{1,0:T(8,128)(2,1)} %get-tuple-element.57), channel_id=1, source_target_pairs={{0,16},{8,24},{16,0},{24,8},{1,17},{9,25},{17,1},{25,9},{2,18},{10... | collective-permute-start | bytes 580616 | tf_op jit(solution)/shard_map/ppermute | solution.py:512
  77.7 21.9 %collective-permute-start.5 = (bf16[84,1152]{1,0:T(8,128)(2,1)}, bf16[84,1152]{1,0:T(8,128)(2,1)S(1)}, u32[]{:S(2)}, u32[]{:S(2)}) collective-permute-start(bf16[84,1152]{1,0:T(8,128)(2,1)} %get-tuple-element.58), channel_id=1, source_target_pairs={{0,24},{8,16},{16,8},{24,0},{1,25},{9,17},{17,9},{25,1},{2,26},{10... | collective-permute-start | bytes 580616 | tf_op jit(solution)/shard_map/ppermute | solution.py:512
  94.4 15.1 %collective-permute-start.28 = (bf16[84,1152]{1,0:T(8,128)(2,1)S(1)}, bf16[84,1152]{1,0:T(8,128)(2,1)S(1)}, u32[]{:S(2)}, u32[]{:S(2)}) collective-permute-start(bf16[84,1152]{1,0:T(8,128)(2,1)S(1)} %copy-done.45), channel_id=1, source_target_pairs={{0,8},{8,0},{16,24},{24,16},{1,9},{9,1},{17,25},{25,17},{2,10},{10... | collective-permute-start | bytes 580616 | tf_op jit(solution)/shard_map/ppermute | solution.py:512
  95.9 14.5 %collective-permute-start.29 = (bf16[84,1152]{1,0:T(8,128)(2,1)S(1)}, bf16[84,1152]{1,0:T(8,128)(2,1)S(1)}, u32[]{:S(2)}, u32[]{:S(2)}) collective-permute-start(bf16[84,1152]{1,0:T(8,128)(2,1)S(1)} %copy-done.43), channel_id=1, source_target_pairs={{0,16},{8,24},{16,0},{24,8},{1,17},{9,25},{17,1},{25,9},{2,18},{10... | collective-permute-start | bytes 580616 | tf_op jit(solution)/shard_map/ppermute | solution.py:512
  97.1 15.0 %collective-permute-start.30 = (bf16[84,1152]{1,0:T(8,128)(2,1)S(1)}, bf16[84,1152]{1,0:T(8,128)(2,1)S(1)}, u32[]{:S(2)}, u32[]{:S(2)}) collective-permute-start(bf16[84,1152]{1,0:T(8,128)(2,1)S(1)} %copy-done.41), channel_id=1, source_target_pairs={{0,24},{8,16},{16,8},{24,0},{1,25},{9,17},{17,9},{25,1},{2,26},{10... | collective-permute-start | bytes 580616 | tf_op jit(solution)/shard_map/ppermute | solution.py:512
  98.1 15.1 %collective-permute-start.12 = (bf16[84,1152]{1,0:T(8,128)(2,1)}, bf16[84,1152]{1,0:T(8,128)(2,1)S(1)}, u32[]{:S(2)}, u32[]{:S(2)}) collective-permute-start(bf16[84,1152]{1,0:T(8,128)(2,1)} %get-tuple-element.69), channel_id=1, source_target_pairs={{0,8},{8,0},{16,24},{24,16},{1,9},{9,1},{17,25},{25,17},{2,10},{10... | collective-permute-start | bytes 580616 | tf_op jit(solution)/shard_map/ppermute | solution.py:512
  99.6 14.6 %collective-permute-start.13 = (bf16[84,1152]{1,0:T(8,128)(2,1)}, bf16[84,1152]{1,0:T(8,128)(2,1)S(1)}, u32[]{:S(2)}, u32[]{:S(2)}) collective-permute-start(bf16[84,1152]{1,0:T(8,128)(2,1)} %get-tuple-element.70), channel_id=1, source_target_pairs={{0,16},{8,24},{16,0},{24,8},{1,17},{9,25},{17,1},{25,9},{2,18},{10... | collective-permute-start | bytes 580616 | tf_op jit(solution)/shard_map/ppermute | solution.py:512
  109.5 10.5 %collective-permute-start.14 = (bf16[84,1152]{1,0:T(8,128)(2,1)S(1)}, bf16[84,1152]{1,0:T(8,128)(2,1)S(1)}, u32[]{:S(2)}, u32[]{:S(2)}) collective-permute-start(bf16[84,1152]{1,0:T(8,128)(2,1)S(1)} %copy-done.38), channel_id=1, source_target_pairs={{0,24},{8,16},{16,8},{24,0},{1,25},{9,17},{17,9},{25,1},{2,26},{10... | collective-permute-start | bytes 580616 | tf_op jit(solution)/shard_map/ppermute | solution.py:512
  110.5 11.8 %collective-permute-start.18 = (bf16[84,1152]{1,0:T(8,128)(2,1)S(1)}, bf16[84,1152]{1,0:T(8,128)(2,1)S(1)}, u32[]{:S(2)}, u32[]{:S(2)}) collective-permute-start(bf16[84,1152]{1,0:T(8,128)(2,1)S(1)} %copy-done.46), channel_id=1, source_target_pairs={{0,8},{8,0},{16,24},{24,16},{1,9},{9,1},{17,25},{25,17},{2,10},{10... | collective-permute-start | bytes 580616 | tf_op jit(solution)/shard_map/ppermute | solution.py:512
  112.1 12.4 %collective-permute-start.19 = (bf16[84,1152]{1,0:T(8,128)(2,1)S(1)}, bf16[84,1152]{1,0:T(8,128)(2,1)S(1)}, u32[]{:S(2)}, u32[]{:S(2)}) collective-permute-start(bf16[84,1152]{1,0:T(8,128)(2,1)S(1)} %copy-done.44), channel_id=1, source_target_pairs={{0,16},{8,24},{16,0},{24,8},{1,17},{9,25},{17,1},{25,9},{2,18},{10... | collective-permute-start | bytes 580616 | tf_op jit(solution)/shard_map/ppermute | solution.py:512
  113.2 14.1 %collective-permute-start.20 = (bf16[84,1152]{1,0:T(8,128)(2,1)S(1)}, bf16[84,1152]{1,0:T(8,128)(2,1)S(1)}, u32[]{:S(2)}, u32[]{:S(2)}) collective-permute-start(bf16[84,1152]{1,0:T(8,128)(2,1)S(1)} %copy-done.42), channel_id=1, source_target_pairs={{0,24},{8,16},{16,8},{24,0},{1,25},{9,17},{17,9},{25,1},{2,26},{10... | collective-permute-start | bytes 580616 | tf_op jit(solution)/shard_map/ppermute | solution.py:512
  114.2 16.8 %collective-permute-start.24 = (bf16[84,1152]{1,0:T(8,128)(2,1)}, bf16[84,1152]{1,0:T(8,128)(2,1)S(1)}, u32[]{:S(2)}, u32[]{:S(2)}) collective-permute-start(bf16[84,1152]{1,0:T(8,128)(2,1)} %get-tuple-element.87), channel_id=1, source_target_pairs={{0,8},{8,0},{16,24},{24,16},{1,9},{9,1},{17,25},{25,17},{2,10},{10... | collective-permute-start | bytes 580616 | tf_op jit(solution)/shard_map/ppermute | solution.py:512
  120.1 25.0 %collective-permute-start.25 = (bf16[84,1152]{1,0:T(8,128)(2,1)}, bf16[84,1152]{1,0:T(8,128)(2,1)S(1)}, u32[]{:S(2)}, u32[]{:S(2)}) collective-permute-start(bf16[84,1152]{1,0:T(8,128)(2,1)} %get-tuple-element.88), channel_id=1, source_target_pairs={{0,16},{8,24},{16,0},{24,8},{1,17},{9,25},{17,1},{25,9},{2,18},{10... | collective-permute-start | bytes 580616 | tf_op jit(solution)/shard_map/ppermute | solution.py:512
  122.3 24.4 %collective-permute-start.26 = (bf16[84,1152]{1,0:T(8,128)(2,1)}, bf16[84,1152]{1,0:T(8,128)(2,1)S(1)}, u32[]{:S(2)}, u32[]{:S(2)}) collective-permute-start(bf16[84,1152]{1,0:T(8,128)(2,1)} %get-tuple-element.89), channel_id=1, source_target_pairs={{0,24},{8,16},{16,8},{24,0},{1,25},{9,17},{17,9},{25,1},{2,26},{10... | collective-permute-start | bytes 580616 | tf_op jit(solution)/shard_map/ppermute | solution.py:512
  124.5 26.9 %collective-permute-start.6 = (bf16[84,1152]{1,0:T(8,128)(2,1)}, bf16[84,1152]{1,0:T(8,128)(2,1)S(1)}, u32[]{:S(2)}, u32[]{:S(2)}) collective-permute-start(bf16[84,1152]{1,0:T(8,128)(2,1)} %get-tuple-element.60), channel_id=1, source_target_pairs={{0,8},{8,0},{16,24},{24,16},{1,9},{9,1},{17,25},{25,17},{2,10},{10... | collective-permute-start | bytes 580616 | tf_op jit(solution)/shard_map/ppermute | solution.py:512
  127.3 25.3 %collective-permute-start.7 = (bf16[84,1152]{1,0:T(8,128)(2,1)}, bf16[84,1152]{1,0:T(8,128)(2,1)S(1)}, u32[]{:S(2)}, u32[]{:S(2)}) collective-permute-start(bf16[84,1152]{1,0:T(8,128)(2,1)} %get-tuple-element.61), channel_id=1, source_target_pairs={{0,16},{8,24},{16,0},{24,8},{1,17},{9,25},{17,1},{25,9},{2,18},{10... | collective-permute-start | bytes 580616 | tf_op jit(solution)/shard_map/ppermute | solution.py:512
  131.0 21.6 %collective-permute-start.8 = (bf16[84,1152]{1,0:T(8,128)(2,1)}, bf16[84,1152]{1,0:T(8,128)(2,1)S(1)}, u32[]{:S(2)}, u32[]{:S(2)}) collective-permute-start(bf16[84,1152]{1,0:T(8,128)(2,1)} %get-tuple-element.62), channel_id=1, source_target_pairs={{0,24},{8,16},{16,8},{24,0},{1,25},{9,17},{17,9},{25,1},{2,26},{10... | collective-permute-start | bytes 580616 | tf_op jit(solution)/shard_map/ppermute | solution.py:512
  145.1 14.2 %collective-permute-start.31 = (bf16[84,1152]{1,0:T(8,128)(2,1)}, bf16[84,1152]{1,0:T(8,128)(2,1)S(1)}, u32[]{:S(2)}, u32[]{:S(2)}) collective-permute-start(bf16[84,1152]{1,0:T(8,128)(2,1)} %get-tuple-element.96), channel_id=1, source_target_pairs={{0,8},{8,0},{16,24},{24,16},{1,9},{9,1},{17,25},{25,17},{2,10},{10... | collective-permute-start | bytes 580616 | tf_op jit(solution)/shard_map/ppermute | solution.py:512
  146.7 12.6 %collective-permute-start.32 = (bf16[84,1152]{1,0:T(8,128)(2,1)}, bf16[84,1152]{1,0:T(8,128)(2,1)S(1)}, u32[]{:S(2)}, u32[]{:S(2)}) collective-permute-start(bf16[84,1152]{1,0:T(8,128)(2,1)} %get-tuple-element.97), channel_id=1, source_target_pairs={{0,16},{8,24},{16,0},{24,8},{1,17},{9,25},{17,1},{25,9},{2,18},{10... | collective-permute-start | bytes 580616 | tf_op jit(solution)/shard_map/ppermute | solution.py:512
  151.3 7.9 %collective-permute-start.33 = (bf16[84,1152]{1,0:T(8,128)(2,1)}, bf16[84,1152]{1,0:T(8,128)(2,1)S(1)}, u32[]{:S(2)}, u32[]{:S(2)}) collective-permute-start(bf16[84,1152]{1,0:T(8,128)(2,1)} %get-tuple-element.98), channel_id=1, source_target_pairs={{0,24},{8,16},{16,8},{24,0},{1,25},{9,17},{17,9},{25,1},{2,26},{10... | collective-permute-start | bytes 580616 | tf_op jit(solution)/shard_map/ppermute | solution.py:512
  164.8 7.0 %collective-permute-start.35 = (bf16[96,64]{1,0:T(8,128)(2,1)S(1)}, bf16[96,64]{1,0:T(8,128)(2,1)S(1)}, u32[]{:S(2)}, u32[]{:S(2)}) collective-permute-start(bf16[96,64]{1,0:T(8,128)(2,1)S(1)} %get-tuple-element.114), channel_id=1, source_target_pairs={{1,0},{2,1},{3,2},{0,3},{5,4},{6,5},{7,6},{4,7},{9,8},{10,9},{11,1... | collective-permute-start | bytes 36872 | tf_op jit(solution)/shard_map/ppermute | solution.py:113
  166.8 5.6 %collective-permute-start.34 = (bf16[96,64]{1,0:T(8,128)(2,1)S(1)}, bf16[96,64]{1,0:T(8,128)(2,1)S(1)}, u32[]{:S(2)}, u32[]{:S(2)}) collective-permute-start(bf16[96,64]{1,0:T(8,128)(2,1)S(1)} %get-tuple-element.113), channel_id=1, source_target_pairs={{0,1},{1,2},{2,3},{3,0},{4,5},{5,6},{6,7},{7,4},{8,9},{9,10},{10,1... | collective-permute-start | bytes 36872 | tf_op jit(solution)/shard_map/ppermute | solution.py:112
  172.5 3.5 %collective-permute-start.36 = (bf16[96,512]{1,0:T(8,128)(2,1)S(1)}, bf16[96,512]{1,0:T(8,128)(2,1)S(1)}, u32[]{:S(2)}, u32[]{:S(2)}) collective-permute-start(bf16[96,512]{1,0:T(8,128)(2,1)S(1)} %get-tuple-element.110), channel_id=1, source_target_pairs={{0,4},{1,5},{2,6},{3,7},{8,12},{9,13},{10,14},{11,15},{16,20},{17,... | collective-permute-start | bytes 294920 | tf_op jit(solution)/shard_map/ppermute | solution.py:121
  173.8 3.2 %collective-permute-start.37 = (bf16[96,512]{1,0:T(8,128)(2,1)S(1)}, bf16[96,512]{1,0:T(8,128)(2,1)S(1)}, u32[]{:S(2)}, u32[]{:S(2)}) collective-permute-start(bf16[96,512]{1,0:T(8,128)(2,1)S(1)} %get-tuple-element.109), channel_id=1, source_target_pairs={{4,0},{5,1},{6,2},{7,3},{12,8},{13,9},{14,10},{15,11},{20,16},{21,... | collective-permute-start | bytes 294920 | tf_op jit(solution)/shard_map/ppermute | solution.py:124
  238.3 1.9 collective-permute-start.38
  241.3 4.9 %collective-permute-start.39 = (f32[24,864]{1,0:T(8,128)S(1)}, f32[24,864]{1,0:T(8,128)S(1)}, u32[]{:S(2)}, u32[]{:S(2)}) collective-permute-start(f32[24,864]{1,0:T(8,128)S(1)} %slice_select_fusion.1), channel_id=1, source_target_pairs={{0,8},{8,0},{16,24},{24,16},{1,9},{9,1},{17,25},{25,17},{2,10},{10... | collective-permute-start | bytes 248840 | tf_op jit(solution)/shard_map/ppermute | solution.py:462
  246.2 4.6 %collective-permute-start.40 = (f32[24,864]{1,0:T(8,128)S(1)}, f32[24,864]{1,0:T(8,128)S(1)}, u32[]{:S(2)}, u32[]{:S(2)}) collective-permute-start(f32[24,864]{1,0:T(8,128)S(1)} %select_add_fusion.1), channel_id=1, source_target_pairs={{0,16},{8,24},{16,0},{24,8},{1,17},{9,25},{17,1},{25,9},{2,18},{10... | collective-permute-start | bytes 248840 | tf_op jit(solution)/shard_map/ppermute | solution.py:465
  250.8 4.6 %collective-permute-start.41 = (f32[24,864]{1,0:T(8,128)S(1)}, f32[24,864]{1,0:T(8,128)S(1)}, u32[]{:S(2)}, u32[]{:S(2)}) collective-permute-start(f32[24,864]{1,0:T(8,128)S(1)} %add.35), channel_id=1, source_target_pairs={{0,1},{1,0},{2,3},{3,2},{4,5},{5,4},{6,7},{7,6},{8,9},{9,8},{10,11... | collective-permute-start | bytes 248840 | tf_op jit(solution)/shard_map/ppermute | solution.py:465
  255.3 6.4 %collective-permute-start.42 = (f32[24,864]{1,0:T(8,128)S(1)}, f32[24,864]{1,0:T(8,128)S(1)}, u32[]{:S(2)}, u32[]{:S(2)}) collective-permute-start(f32[24,864]{1,0:T(8,128)S(1)} %add.36), channel_id=1, source_target_pairs={{0,2},{1,3},{2,0},{3,1},{4,6},{5,7},{6,4},{7,5},{8,10},{9,11},{10,... | collective-permute-start | bytes 248840 | tf_op jit(solution)/shard_map/ppermute | solution.py:465
  261.7 4.6 %collective-permute-start.43 = (f32[24,864]{1,0:T(8,128)S(1)}, f32[24,864]{1,0:T(8,128)S(1)}, u32[]{:S(2)}, u32[]{:S(2)}) collective-permute-start(f32[24,864]{1,0:T(8,128)S(1)} %add.37), channel_id=1, source_target_pairs={{0,8},{8,0},{16,24},{24,16},{1,9},{9,1},{17,25},{25,17},{2,10},{10... | collective-permute-start | bytes 248840 | tf_op jit(solution)/shard_map/ppermute | solution.py:468
  266.3 1.5 collective-permute-start.44
  (52 other events, 645.0 us)
